TPU v7x, 32 devices: a whole 2x2x4 slice. The times are simulated.
32 devices in a mesh: dp: 8 (over y, x, core), group: 4 (over z).
Axes of the slice: x: 2, y: 2, z: 4, core: 2. Of those that a mesh axis runs over, the one named last changes fastest.
Arguments:
- tokens: bfloat16 [32768, 768], P(('dp', 'group')), may hold values from -6 to 6
- cotangent: bfloat16 [32768, 768], P(('dp', 'group')), may hold values from -6 to 6
- seq_lens: int32 [32, 4], P(('dp', 'group')), may hold values from 0 to 1024, as said below
- w_qkv: float32 [1769472], P(('dp', 'group')), may hold values from -0.21875 to 0.21875
- w_out: float32 [589824], P(('dp', 'group')), may hold values from -1.75 to 1.75
- w_up: float32 [2359296], P(('dp', 'group')), may hold values from -0.21875 to 0.21875
- w_down: float32 [2359296], P(('dp', 'group')), may hold values from -0.109375 to 0.109375
- vectors: float32 [9984], P(('dp', 'group')), may hold values from -0.4 to 1.3, as said below
- first_qkv: float32 [1769472], P(('dp', 'group')), may hold values from -128 to 128
- first_out: float32 [589824], P(('dp', 'group')), may hold values from -12 to 12
- first_up: float32 [2359296], P(('dp', 'group')), may hold values from -32 to 32
- first_down: float32 [2359296], P(('dp', 'group')), may hold values from -64 to 64
- first_vec: float32 [9984], P(('dp', 'group')), may hold values from -256 to 256
- second_qkv: float32 [1769472], P(('dp', 'group')), may hold values from 16.384 to 262.144
- second_out: float32 [589824], P(('dp', 'group')), may hold values from 0.16384 to 2.62144
- second_up: float32 [2359296], P(('dp', 'group')), may hold values from 0.98304 to 16.384
- second_down: float32 [2359296], P(('dp', 'group')), may hold values from 4.096 to 65.536
- second_vec: float32 [9984], P(('dp', 'group')), may hold values from 65.536 to 1048.576
Outputs:
- block_out: bfloat16 [32768, 768], P(('dp', 'group'))
- input_grad: float32 [32768, 768], P(('dp', 'group'))
- new_w_qkv: float32 [1769472], P(('dp', 'group'))
- new_w_out: float32 [589824], P(('dp', 'group'))
- new_w_up: float32 [2359296], P(('dp', 'group'))
- new_w_down: float32 [2359296], P(('dp', 'group'))
- new_vectors: float32 [9984], P(('dp', 'group'))
- new_first_qkv: float32 [1769472], P(('dp', 'group'))
- new_first_out: float32 [589824], P(('dp', 'group'))
- new_first_up: float32 [2359296], P(('dp', 'group'))
- new_first_down: float32 [2359296], P(('dp', 'group'))
- new_first_vec: float32 [9984], P(('dp', 'group'))
- new_second_qkv: float32 [1769472], P(('dp', 'group'))
- new_second_out: float32 [589824], P(('dp', 'group'))
- new_second_up: float32 [2359296], P(('dp', 'group'))
- new_second_down: float32 [2359296], P(('dp', 'group'))
- new_second_vec: float32 [9984], P(('dp', 'group'))
Inputs may be any that keep to these rules, and one draw needn't show every extreme that they name: `seq_lens`: row r lists, in order, the lengths of the sequences packed into the rows of device r of dp+group (dp slowest); its nonzero entries come first and sum to at most 1024; some row begins with a sequence of 1024 tokens and sums to exactly 1024. `vectors`: entries 0 to 2 * 768 - 1 (the gains) lie between 0.7 and 1.3; the others between -0.4 and 0.4.
All inputs are finite; a program needn't handle non-finite values.
Results may differ from a plain program's by a relative error of at most 0.012.
Values may be sent and summed in bfloat16 or wider, within the bound.
A program may use at most 192 MiB of HBM per device.

v0:
```python
import jax
import jax.numpy as jnp
from jax import lax
from jax.sharding import PartitionSpec as P

D = 768
HEADS = 12
HEAD = 64
ROT = 16
FF = 3072
TOK_DEV = 1024
BLOCK = 512
STEP = 10


norm_eps = 1e-05
beta_first = 0.9
beta_second = 0.999
learn_rate = 0.05
vector_rate = 0.3
weight_decay = 0.1
adam_eps = 1e-08
masked_value = -1e30
rotary_base = 10000.0


def norm_parts(inputs, gain, shift):
    average = jnp.mean(inputs, axis=-1, keepdims=True)
    centred = inputs - average
    spread = jnp.mean(centred * centred, axis=-1, keepdims=True)
    scaled = lax.rsqrt(spread + norm_eps)
    normal = centred * scaled
    return (normal * gain + shift, normal, scaled)


def norm_back(upstream, normal, scaled, gain):
    weighted = upstream * gain
    inner = weighted - jnp.mean(weighted, axis=-1, keepdims=True)
    inner = inner - normal * jnp.mean(weighted * normal, axis=-1, keepdims=True)
    return (scaled * inner, jnp.sum(upstream * normal, axis=0), jnp.sum(upstream, axis=0))


def packing(lengths):
    seq_ends = jnp.cumsum(lengths)
    row_ids = jnp.arange(TOK_DEV, dtype=jnp.int32)
    passed = row_ids[:, None] >= seq_ends[None, :]
    document = jnp.sum(passed.astype(jnp.int32), axis=1)
    begins = jnp.max(jnp.where(passed, seq_ends[None, :], 0), axis=1)
    return (document, row_ids - begins, row_ids < seq_ends[-1])


def rotate(inputs, cosines, sines):
    half_rot = ROT // 2
    turned = inputs[..., :ROT]
    swapped = jnp.concatenate([-turned[..., half_rot:], turned[..., :half_rot]], axis=-1)
    turned = turned * cosines[:, None, :] + swapped * sines[:, None, :]
    return jnp.concatenate([turned, inputs[..., ROT:]], axis=-1)


def unrotate(upstream, cosines, sines):
    half_rot = ROT // 2
    turned = upstream[..., :ROT]
    tilted = turned * sines[:, None, :]
    back = turned * cosines[:, None, :] + jnp.concatenate(
        [tilted[..., half_rot:], -tilted[..., :half_rot]], axis=-1
    )
    return jnp.concatenate([back, upstream[..., ROT:]], axis=-1)


def block_scores(offset, queries, key_rows, document):
    query_rows = lax.dynamic_slice_in_dim(queries, offset, BLOCK, 0)
    query_docs = lax.dynamic_slice_in_dim(document, offset, BLOCK, 0)
    raw = jnp.einsum(
        "qhd,khd->hqk", query_rows, key_rows, preferred_element_type=jnp.float32
    ) * HEAD ** (-0.5)
    row_ids = offset + jnp.arange(BLOCK, dtype=jnp.int32)
    col_ids = jnp.arange(key_rows.shape[0], dtype=jnp.int32)
    allowed = (query_docs[:, None] == document[None, :]) & (col_ids[None, :] <= row_ids[:, None])
    return jnp.where(allowed[None], raw, masked_value)


def adam_step(weight, gradient, moment_one, moment_two, decay_rate, step_rate):
    moment_one = beta_first * moment_one + (1.0 - beta_first) * gradient
    moment_two = beta_second * moment_two + (1.0 - beta_second) * gradient * gradient
    first_hat = moment_one / (1.0 - beta_first**STEP)
    second_hat = moment_two / (1.0 - beta_second**STEP)
    weight = weight - step_rate * (
        first_hat / (jnp.sqrt(second_hat) + adam_eps) + decay_rate * weight
    )
    return (weight, moment_one, moment_two)


def per_device(
    tokens,
    cotangent,
    seq_lens,
    w_qkv,
    w_out,
    w_up,
    w_down,
    vectors,
    first_qkv,
    first_out,
    first_up,
    first_down,
    first_vec,
    second_qkv,
    second_out,
    second_up,
    second_down,
    second_vec,
):
    gathered = (
        lax.all_gather(w_qkv.astype(jnp.bfloat16), ("dp", "group"), axis=0, tiled=True),
        lax.all_gather(w_out.astype(jnp.bfloat16), ("dp", "group"), axis=0, tiled=True),
        lax.all_gather(w_up.astype(jnp.bfloat16), ("dp", "group"), axis=0, tiled=True),
        lax.all_gather(w_down.astype(jnp.bfloat16), ("dp", "group"), axis=0, tiled=True),
        lax.all_gather(vectors.astype(jnp.bfloat16), ("dp", "group"), axis=0, tiled=True),
    )
    weight_qkv = gathered[0].reshape(D, 3 * D)
    weight_out = gathered[1].reshape(D, D)
    weight_up = gathered[2].reshape(D, FF)
    weight_down = gathered[3].reshape(FF, D)
    packed = gathered[4].astype(jnp.float32)
    gain_one = packed[0:D]
    gain_two = packed[D : 2 * D]
    shift_one = packed[2 * D : 3 * D]
    shift_two = packed[3 * D : 4 * D]
    bias_qkv = packed[4 * D : 7 * D]
    bias_out = packed[7 * D : 8 * D]
    bias_up = packed[8 * D : 8 * D + FF]
    bias_down = packed[8 * D + FF :]
    document, position, live_rows = packing(seq_lens[0])
    half_rot = ROT // 2
    inverse = rotary_base ** (-(2.0 * jnp.arange(half_rot, dtype=jnp.float32)) / ROT)
    phases = position.astype(jnp.float32)[:, None] * inverse
    phases = jnp.concatenate([phases, phases], axis=-1)
    cosines = jnp.cos(phases)
    sines = jnp.sin(phases)
    scaling = HEAD ** (-0.5)
    inputs = tokens.astype(jnp.float32)
    normed_one, normal_one, scaled_one = norm_parts(inputs, gain_one, shift_one)
    normed_two, normal_two, scaled_two = norm_parts(inputs, gain_two, shift_two)
    normed_one = normed_one.astype(jnp.bfloat16)
    normed_two = normed_two.astype(jnp.bfloat16)
    projected = jnp.dot(normed_one, weight_qkv, preferred_element_type=jnp.float32) + bias_qkv
    projected = projected.reshape(TOK_DEV, HEADS, 3 * HEAD)
    queries = rotate(projected[..., :HEAD], cosines, sines).astype(jnp.bfloat16)
    key_rows = rotate(projected[..., HEAD : 2 * HEAD], cosines, sines).astype(jnp.bfloat16)
    values = projected[..., 2 * HEAD :].astype(jnp.bfloat16)
    offsets = jnp.arange(TOK_DEV // BLOCK, dtype=jnp.int32) * BLOCK

    def forward_block(offset):
        scores = block_scores(offset, queries, key_rows, document)
        highest = jnp.max(scores, axis=-1, keepdims=True)
        expanded = jnp.exp(scores - highest)
        totals = jnp.sum(expanded, axis=-1, keepdims=True)
        probs = (expanded / totals).astype(jnp.bfloat16)
        context_rows = jnp.einsum("hqk,khd->qhd", probs, values, preferred_element_type=jnp.float32)
        return (context_rows, (highest + jnp.log(totals))[..., 0])

    context, logsums = lax.map(forward_block, offsets)
    context = context.reshape(TOK_DEV, D).astype(jnp.bfloat16)
    attended = jnp.dot(context, weight_out, preferred_element_type=jnp.float32) + bias_out
    hidden = jnp.dot(normed_two, weight_up, preferred_element_type=jnp.float32) + bias_up
    activation, gelu_back = jax.vjp(lambda entry: jax.nn.gelu(entry, approximate=False), hidden)
    activated = activation.astype(jnp.bfloat16)
    result = (
        inputs
        + attended
        + jnp.dot(activated, weight_down, preferred_element_type=jnp.float32)
        + bias_down
    )
    seed_rows = jnp.where(live_rows[:, None], cotangent, jnp.zeros_like(cotangent))
    seed_float = seed_rows.astype(jnp.float32)
    grad_down = jnp.einsum("tf,td->fd", activated, seed_rows, preferred_element_type=jnp.float32)
    grad_out = jnp.einsum("tc,td->cd", context, seed_rows, preferred_element_type=jnp.float32)
    grad_act = jnp.einsum("td,fd->tf", seed_rows, weight_down, preferred_element_type=jnp.float32)
    grad_hidden = gelu_back(grad_act)[0].astype(jnp.bfloat16)
    grad_up = jnp.einsum("td,tf->df", normed_two, grad_hidden, preferred_element_type=jnp.float32)
    grad_two = jnp.einsum("tf,df->td", grad_hidden, weight_up, preferred_element_type=jnp.float32)
    grad_context = jnp.einsum(
        "td,cd->tc", seed_rows, weight_out, preferred_element_type=jnp.float32
    )
    grad_context = grad_context.astype(jnp.bfloat16).reshape(TOK_DEV, HEADS, HEAD)

    def backward_block(running, items):
        grad_keys, grad_values = running
        offset, logsum_rows = items
        scores = block_scores(offset, queries, key_rows, document)
        probs = jnp.exp(scores - logsum_rows[..., None])
        upstream = lax.dynamic_slice_in_dim(grad_context, offset, BLOCK, 0)
        query_rows = lax.dynamic_slice_in_dim(queries, offset, BLOCK, 0)
        dprob = jnp.einsum("qhd,khd->hqk", upstream, values, preferred_element_type=jnp.float32)
        inner = jnp.sum(probs * dprob, axis=-1, keepdims=True)
        grad_scores = (probs * (dprob - inner)).astype(jnp.bfloat16)
        grad_rows = (
            jnp.einsum("hqk,khd->qhd", grad_scores, key_rows, preferred_element_type=jnp.float32)
            * scaling
        )
        grad_keys = (
            grad_keys
            + jnp.einsum(
                "hqk,qhd->khd", grad_scores, query_rows, preferred_element_type=jnp.float32
            )
            * scaling
        )
        grad_values = grad_values + jnp.einsum(
            "hqk,qhd->khd", probs.astype(jnp.bfloat16), upstream, preferred_element_type=jnp.float32
        )
        return ((grad_keys, grad_values), grad_rows)

    empty = jnp.zeros((TOK_DEV, HEADS, HEAD), jnp.float32)
    (grad_keys, grad_values), grad_queries = lax.scan(
        backward_block, (empty, empty), (offsets, logsums)
    )
    grad_queries = grad_queries.reshape(TOK_DEV, HEADS, HEAD)
    grad_projected = jnp.concatenate(
        [unrotate(grad_queries, cosines, sines), unrotate(grad_keys, cosines, sines), grad_values],
        axis=-1,
    )
    grad_projected = grad_projected.reshape(TOK_DEV, 3 * D).astype(jnp.bfloat16)
    grad_qkv = jnp.einsum(
        "td,te->de", normed_one, grad_projected, preferred_element_type=jnp.float32
    )
    grad_one = jnp.einsum(
        "te,de->td", grad_projected, weight_qkv, preferred_element_type=jnp.float32
    )
    input_one, gain_grad_one, shift_grad_one = norm_back(grad_one, normal_one, scaled_one, gain_one)
    input_two, gain_grad_two, shift_grad_two = norm_back(grad_two, normal_two, scaled_two, gain_two)
    input_grad = seed_float + input_one + input_two
    seed_total = jnp.sum(seed_float, axis=0)
    grad_vec = jnp.concatenate(
        [
            gain_grad_one,
            gain_grad_two,
            shift_grad_one,
            shift_grad_two,
            jnp.sum(grad_projected.astype(jnp.float32), axis=0),
            seed_total,
            jnp.sum(grad_hidden.astype(jnp.float32), axis=0),
            seed_total,
        ]
    )
    summed = (
        lax.psum_scatter(grad_qkv.reshape(-1), ("dp", "group"), scatter_dimension=0, tiled=True),
        lax.psum_scatter(grad_out.reshape(-1), ("dp", "group"), scatter_dimension=0, tiled=True),
        lax.psum_scatter(grad_up.reshape(-1), ("dp", "group"), scatter_dimension=0, tiled=True),
        lax.psum_scatter(grad_down.reshape(-1), ("dp", "group"), scatter_dimension=0, tiled=True),
        lax.psum_scatter(grad_vec, ("dp", "group"), scatter_dimension=0, tiled=True),
    )
    masters = (w_qkv, w_out, w_up, w_down, vectors)
    firsts = (first_qkv, first_out, first_up, first_down, first_vec)
    seconds = (second_qkv, second_out, second_up, second_down, second_vec)
    decays = (weight_decay, weight_decay, weight_decay, weight_decay, 0.0)
    rates = (learn_rate, learn_rate, learn_rate, learn_rate, vector_rate)
    updated = [
        adam_step(weight, gradient, moment_one, moment_two, decay_rate, step_rate)
        for weight, gradient, moment_one, moment_two, decay_rate, step_rate in zip(
            masters, summed, firsts, seconds, decays, rates
        )
    ]
    return (
        result.astype(jnp.bfloat16),
        input_grad,
        updated[0][0],
        updated[1][0],
        updated[2][0],
        updated[3][0],
        updated[4][0],
        updated[0][1],
        updated[1][1],
        updated[2][1],
        updated[3][1],
        updated[4][1],
        updated[0][2],
        updated[1][2],
        updated[2][2],
        updated[3][2],
        updated[4][2],
    )


def solution(mesh):
    placed = (
        P(("dp", "group"), None),
        P(("dp", "group"), None),
        P(("dp", "group"), None),
        P(("dp", "group")),
        P(("dp", "group")),
        P(("dp", "group")),
        P(("dp", "group")),
        P(("dp", "group")),
        P(("dp", "group")),
        P(("dp", "group")),
        P(("dp", "group")),
        P(("dp", "group")),
        P(("dp", "group")),
        P(("dp", "group")),
        P(("dp", "group")),
        P(("dp", "group")),
        P(("dp", "group")),
        P(("dp", "group")),
    )
    return jax.shard_map(
        per_device,
        mesh=mesh,
        in_specs=placed,
        out_specs=(
            P(("dp", "group"), None),
            P(("dp", "group"), None),
            P(("dp", "group")),
            P(("dp", "group")),
            P(("dp", "group")),
            P(("dp", "group")),
            P(("dp", "group")),
            P(("dp", "group")),
            P(("dp", "group")),
            P(("dp", "group")),
            P(("dp", "group")),
            P(("dp", "group")),
            P(("dp", "group")),
            P(("dp", "group")),
            P(("dp", "group")),
            P(("dp", "group")),
            P(("dp", "group")),
        ),
        check_vma=False,
    )
```

profile of v0, /device:TPU:0, one launch (start us, length us, event | category | flops | bytes accessed | tf_op | source)
XLA Modules:
  0.0 1077.5 jit_solution(16450977775475290429)
XLA Ops:
  15.1 42.2 %all-reduce = bf16[9984]{0:T(1024)(128)(2,1)S(1)} all-reduce(bf16[9984]{0:T(1024)(128)(2,1)S(1)} %dynamic-update-slice), channel_id=1, replica_groups=mesh['dp'=8,'group'=4] {'dp','group'}, use_global_device_ids=true, to_apply=%add | all-reduce | flops 9984 | bytes 39936
  75.7 55.0 %all-gather.5.cloned.1.call-done = bf16[1769472]{0:T(1024)(128)(2,1)} async-done(((bf16[55296]{0:T(1024)(128)(2,1)}), bf16[1769472]{0:T(1024)(128)(2,1)}) %all-gather.5.cloned.1.call-update) | async-done | bytes 3538960 | tf_op jit(solution)/shard_map/all_gather | solution.py:114
  138.3 8.6 convolution_add_fusion
  147.0 9.7 copy.48
  166.2 78.7 %while.27 = (s32[]{:T(128)}, bf16[2,512,12,64]{1,3,2,0:T(8,128)(2,1)}, f32[2,12,512]{2,1,0:T(8,128)S(1)}, s32[2]{0:T(128)S(1)}, s32[1024]{0:T(1024)S(1)}, /*inde...) while((s32[]{:T(128)}, ...), condition=%wide.region_8.9_spmd, body=%wide.region_5.8_spmd.sunk | while | flops 1687677440 | bytes 190290672 | solution.py:162
  170.4 11.2 %fusion.136 = (f32[12,512]{1,0:T(8,128)S(1)}, f32[12,512,1024]{2,1,0:T(8,128)}) fusion(pred[512,1024]{1,0:T(8,128)(4,1)S(1)} %fusion.135, bf16[1024,12,64]{0,2,1:T(8,128)(2,1)S(1)} %get-tuple-element.419, bf16[1024,12,64]{0,2,1:T(8,128)(2,1)S(1)} %get-tuple-element.418, s32[]{:T(128)S(6)} %select_n.74), kind=kOutput, calls=%fused_computation.3.clone.1 | convolution fusion | flops 824174592 | bytes 28073988 | tf_op jit(solution)/shard_map/while/body/eval_jaxpr/qhd,khd->hqk/dot_general | solution.py:73
  181.7 12.5 %fusion.137 = f32[12,512]{1,0:T(8,128)S(1)} fusion(f32[12,512,1024]{2,1,0:T(8,128)} %get-tuple-element.376, f32[12,512]{1,0:T(8,128)S(1)} %get-tuple-element.377, pred[512,1024]{1,0:T(8,128)(4,1)S(1)} %fusion.135), kind=kLoop, calls=%fused_computation.4.clone.1 | loop fusion | flops 25159680 | bytes 25739264 | tf_op jit(solution)/shard_map/while/body/eval_jaxpr/reduce_sum | solution.py:157
  210.0 10.9 %fusion.136 = (f32[12,512]{1,0:T(8,128)S(1)}, f32[12,512,1024]{2,1,0:T(8,128)}) fusion(pred[512,1024]{1,0:T(8,128)(4,1)S(1)} %fusion.135, bf16[1024,12,64]{0,2,1:T(8,128)(2,1)S(1)} %get-tuple-element.419, bf16[1024,12,64]{0,2,1:T(8,128)(2,1)S(1)} %get-tuple-element.418, s32[]{:T(128)S(6)} %select_n.74), kind=kOutput, calls=%fused_computation.3.clone.1 | convolution fusion | flops 824174592 | bytes 28073988 | tf_op jit(solution)/shard_map/while/body/eval_jaxpr/qhd,khd->hqk/dot_general | solution.py:73
  220.8 12.3 %fusion.137 = f32[12,512]{1,0:T(8,128)S(1)} fusion(f32[12,512,1024]{2,1,0:T(8,128)} %get-tuple-element.376, f32[12,512]{1,0:T(8,128)S(1)} %get-tuple-element.377, pred[512,1024]{1,0:T(8,128)(4,1)S(1)} %fusion.135), kind=kLoop, calls=%fused_computation.4.clone.1 | loop fusion | flops 25159680 | bytes 25739264 | tf_op jit(solution)/shard_map/while/body/eval_jaxpr/reduce_sum | solution.py:157
  244.9 244.1 %while.28 = (s32[]{:T(128)}, f32[1024,12,64]{0,2,1:T(8,128)}, f32[1024,12,64]{0,2,1:T(8,128)}, f32[2,512,12,64]{1,0,3,2:T(2,128)}, s32[2]{0:T(128)S(1)}, /*index...) while((s32[]{:T(128)}, f32[1024,12,64]{0,2,1:T(8,128)}, ...), condition=%wide.region_11.12_spmd.clone, body=%wide.region_9.11_spmd.clone.sunk | while | flops 4126796288 | bytes 242415968 | solution.py:214
  248.9 13.7 %fusion.147 = f32[12,512,1024]{2,1,0:T(8,128)} fusion(bf16[1024,12,64]{0,2,1:T(8,128)(2,1)S(1)} %get-tuple-element.459, bf16[1024,12,64]{0,2,1:T(8,128)(2,1)} %copy-done.4, s32[]{:T(128)S(6)} %select_n.78), kind=kOutput, calls=%fused_computation.31.clone.1 | convolution fusion | flops 805306368 | bytes 27525124 | tf_op jit(solution)/shard_map/while/body/eval_jaxpr/qhd,khd->hqk/dot_general | solution.py:73
  262.6 18.2 %multiply_reduce_fusion.4 = (f32[12,512]{1,0:T(8,128)S(1)}, f32[12,512,1024]{2,1,0:T(8,128)}) fusion(f32[12,512,1024]{2,1,0:T(8,128)} %fusion.147, f32[12,512]{1,0:T(8,128)S(1)} %dynamic-slice_bitcast_fusion.2, pred[512,1024]{1,0:T(8,128)(4,1)S(1)} %fusion.148, bf16[1024,12,64]{0,2,1:T(8,128)(2,1)} %get-tuple-element.462, ...), kind=kOutput, calls=%fused_computation.17.clone.1 | convolution fusion | flops 836757504 | bytes 53264388 | tf_op jit(solution)/shard_map/while/body/eval_jaxpr/qhd,khd->hqk/dot_general | solution.py:194
  280.8 21.2 %multiply_convert_fusion.3 = bf16[12,512,1024]{2,1,0:T(8,128)(2,1)} fusion(f32[12,512,1024]{2,1,0:T(8,128)} %get-tuple-element.389, f32[12,512,1024]{2,1,0:T(8,128)} %fusion.147, f32[12,512]{1,0:T(8,128)S(1)} %get-tuple-element.390, f32[12,512]{1,0:T(8,128)S(1)} %dynamic-slice_bitcast_fusion.2, pred[512,1024]{1,0:T(8,128)(4,1)S(1)} %fusion.148), kind=kLoop, calls=%fused_computation.16.clone.1 | loop fusion | flops 37748736 | bytes 63488000 | tf_op jit(solution)/shard_map/while/body/eval_jaxpr/convert_element_type | solution.py:196
  302.0 9.7 multiply_bitcast_fusion.2
  314.7 28.7 %dynamic_update_slice.19 = f32[2,512,12,64]{1,0,3,2:T(2,128)} dynamic-update-slice(f32[2,512,12,64]{1,0,3,2:T(2,128)} %get-tuple-element.441, f32[1,512,12,64]{1,0,3,2:T(1,128)S(1)} %copy.69, s32[]{:T(128)} %get-tuple-element.438, s32[]{:T(128)} %constant.31.clone.1..sunk.1, s32[]{:T(128)} %constant.31.clone.1..sunk.1, s32[]{:T(128)} %constant.31.clone.1..sunk.1) | dynamic-update-slice | bytes 3145732 | tf_op jit(solution)/shard_map/while/body/jit(dynamic_update_index_in_dim)/dynamic_update_slice | solution.py:162
  343.5 9.1 bitcast_add_fusion.4
  352.5 13.7 %bitcast_add_fusion.5 = f32[1024,12,64]{0,2,1:T(8,128)} fusion(f32[1024,12,64]{0,2,1:T(8,128)} %get-tuple-element.440, f32[12,512,1024]{2,1,0:T(8,128)} %fusion.147, f32[12,512]{1,0:T(8,128)S(1)} %dynamic-slice_bitcast_fusion.2, pred[512,1024]{1,0:T(8,128)(4,1)S(1)} %copy-done.3, pred[]{:T(512)S(6)} %compare.3, ...), kind=kOutput, calls=%fused_computation.22.clone.1 | convolution fusion | flops 832045056 | bytes 32800772 | tf_op jit(solution)/shard_map/while/body/eval_jaxpr/hqk,qhd->khd/dot_general | solution.py:208
  370.2 13.3 %fusion.147 = f32[12,512,1024]{2,1,0:T(8,128)} fusion(bf16[1024,12,64]{0,2,1:T(8,128)(2,1)S(1)} %get-tuple-element.459, bf16[1024,12,64]{0,2,1:T(8,128)(2,1)} %copy-done.4, s32[]{:T(128)S(6)} %select_n.78), kind=kOutput, calls=%fused_computation.31.clone.1 | convolution fusion | flops 805306368 | bytes 27525124 | tf_op jit(solution)/shard_map/while/body/eval_jaxpr/qhd,khd->hqk/dot_general | solution.py:73
  383.5 18.2 %multiply_reduce_fusion.4 = (f32[12,512]{1,0:T(8,128)S(1)}, f32[12,512,1024]{2,1,0:T(8,128)}) fusion(f32[12,512,1024]{2,1,0:T(8,128)} %fusion.147, f32[12,512]{1,0:T(8,128)S(1)} %dynamic-slice_bitcast_fusion.2, pred[512,1024]{1,0:T(8,128)(4,1)S(1)} %fusion.148, bf16[1024,12,64]{0,2,1:T(8,128)(2,1)} %get-tuple-element.462, ...), kind=kOutput, calls=%fused_computation.17.clone.1 | convolution fusion | flops 836757504 | bytes 53264388 | tf_op jit(solution)/shard_map/while/body/eval_jaxpr/qhd,khd->hqk/dot_general | solution.py:194
  401.7 21.2 %multiply_convert_fusion.3 = bf16[12,512,1024]{2,1,0:T(8,128)(2,1)} fusion(f32[12,512,1024]{2,1,0:T(8,128)} %get-tuple-element.389, f32[12,512,1024]{2,1,0:T(8,128)} %fusion.147, f32[12,512]{1,0:T(8,128)S(1)} %get-tuple-element.390, f32[12,512]{1,0:T(8,128)S(1)} %dynamic-slice_bitcast_fusion.2, pred[512,1024]{1,0:T(8,128)(4,1)S(1)} %fusion.148), kind=kLoop, calls=%fused_computation.16.clone.1 | loop fusion | flops 37748736 | bytes 63488000 | tf_op jit(solution)/shard_map/while/body/eval_jaxpr/convert_element_type | solution.py:196
  422.9 9.7 multiply_bitcast_fusion.2
  435.7 28.7 %dynamic_update_slice.19 = f32[2,512,12,64]{1,0,3,2:T(2,128)} dynamic-update-slice(f32[2,512,12,64]{1,0,3,2:T(2,128)} %get-tuple-element.441, f32[1,512,12,64]{1,0,3,2:T(1,128)S(1)} %copy.69, s32[]{:T(128)} %get-tuple-element.438, s32[]{:T(128)} %constant.31.clone.1..sunk.1, s32[]{:T(128)} %constant.31.clone.1..sunk.1, s32[]{:T(128)} %constant.31.clone.1..sunk.1) | dynamic-update-slice | bytes 3145732 | tf_op jit(solution)/shard_map/while/body/jit(dynamic_update_index_in_dim)/dynamic_update_slice | solution.py:162
  464.4 9.9 bitcast_add_fusion.4
  474.3 14.6 %bitcast_add_fusion.5 = f32[1024,12,64]{0,2,1:T(8,128)} fusion(f32[1024,12,64]{0,2,1:T(8,128)} %get-tuple-element.440, f32[12,512,1024]{2,1,0:T(8,128)} %fusion.147, f32[12,512]{1,0:T(8,128)S(1)} %dynamic-slice_bitcast_fusion.2, pred[512,1024]{1,0:T(8,128)(4,1)S(1)} %copy-done.3, pred[]{:T(512)S(6)} %compare.3, ...), kind=kOutput, calls=%fused_computation.22.clone.1 | convolution fusion | flops 832045056 | bytes 32800772 | tf_op jit(solution)/shard_map/while/body/eval_jaxpr/hqk,qhd->khd/dot_general | solution.py:208
  535.9 36.3 %multiply_convert_fusion.1 = (bf16[1024,3072]{1,0:T(8,128)(2,1)}, f32[1024,3072]{1,0:T(8,128)}, f32[1024,3072]{1,0:T(8,128)}) fusion(f32[3072]{0:T(1024)S(1)} %copy-done.42, bf16[768,3072]{1,0:T(8,128)(2,1)} %reshape.325, bf16[1024,768]{1,0:T(8,128)(2,1)S(1)} %copy-done.8, f32[768]{0:T(1024)S(1)} %copy-done.46, f32[768]{0:T(1024)S(1)} %copy-done.39, ...), kind=kOutput, calls=%fused_computation.45 | convolution fusion | flops 5044174848 | bytes 37775360 | tf_op jit(solution)/shard_map/dot_general | solution.py:165
  572.2 9.3 reshape.326
  581.5 16.7 %convert_reduce_fusion = (f32[3072]{0:T(1024)S(1)}, bf16[1024,3072]{1,0:T(8,128)(2,1)}) fusion(f32[1024,3072]{1,0:T(8,128)} %get-tuple-element.232, bf16[3072,768]{1,0:T(8,128)(2,1)} %reshape.326, bf16[1024,768]{1,0:T(8,128)(2,1)S(1)} %copy-done.14, pred[1024]{0:T(1024)(128)(4,1)S(1)} %copy-done.52, f32[1024,3072]{1,0:T(8,128)} %get-tuple-element.261, ...), kind=kOutput, calls=%fused_computation.43 | convolution fusion | flops 4886098944 | bytes 37774336 | tf_op jit(solution)/shard_map/td,fd->tf/dot_general | solution.py:178
  620.2 10.7 reshape.332
  634.0 10.1 fusion.93
  656.2 40.4 %all-reduce.5 = f32[9984]{0:T(1024)S(1)} all-reduce(f32[9984]{0:T(1024)S(1)} %constant_dynamic-update-slice_fusion.2), channel_id=6, replica_groups=mesh['dp'=8,'group'=4] {'dp','group'}, use_global_device_ids=true, to_apply=%region_27.28.clone | all-reduce | flops 9984 | bytes 79872
  697.3 8.8 fusion.92
  709.2 354.0 %all-reduce.9.cloned.1.call-done = (f32[1769472]{0:T(1024)}, f32[589824]{0:T(1024)}, f32[2359296]{0:T(1024)}, f32[2359296]{0:T(1024)}) async-done(((f32[1769472]{0:T(1024)}, f32[589824]{0:T(1024)}, f32[2359296]{0:T(1024)}, f32[2359296]{0:T(1024)}), (f32[1769472]{0:T(1024)}, f32[589824]{0:T(1024)}, f32[2359296]{0:T(1024)}, f32[2359296]{0:T(1024)})) %all-reduce.9.cloned.1.call-update) | async-done | bytes 28311568
  (240 shorter events, 175.6 us)
Async XLA Ops:
  7.2 53.1 %copy-start.7 = (bf16[1024,768]{1,0:T(8,128)(2,1)S(1)}, bf16[1024,768]{1,0:T(8,128)(2,1)}, u32[]{:S(2)}) copy-start(bf16[1024,768]{1,0:T(8,128)(2,1)} %param.22) | copy-start | bytes 4718596
  7.2 53.8 %copy-start.53 = (s32[1,4]{1,0:T(1,128)S(1)}, s32[1,4]{1,0:T(1,128)}, u32[]{:S(2)}) copy-start(s32[1,4]{1,0:T(1,128)} %param.24) | copy-start | bytes 52
  7.2 61.1 %all-gather.7.cloned.1.call-start = ((), (), s32[]{:S(2)}) async-start(), calls=%async_computation.1 | async-start | bytes 1216512 | tf_op jit(solution)/shard_map/all_gather | solution.py:115
  8.9 121.8 %all-gather.5.cloned.1.call-start = ((), (), s32[]{:S(2)}) async-start(), calls=%async_computation | async-start | bytes 3649536 | tf_op jit(solution)/shard_map/all_gather | solution.py:114
  10.6 61.1 %copy-start.13 = (bf16[1024,768]{1,0:T(8,128)(2,1)S(1)}, bf16[1024,768]{1,0:T(8,128)(2,1)}, u32[]{:S(2)}) copy-start(bf16[1024,768]{1,0:T(8,128)(2,1)} %param.23) | copy-start | bytes 4718596
  10.6 517.1 %all-gather.9.cloned.1.call-start = ((), (), s32[]{:S(2)}) async-start(), calls=%async_computation.2 | async-start | bytes 4866048 | tf_op jit(solution)/shard_map/all_gather | solution.py:116
  12.4 559.8 %all-gather.11.cloned.1.call-start = ((), (), s32[]{:S(2)}) async-start(), calls=%async_computation.3 | async-start | bytes 4866048 | tf_op jit(solution)/shard_map/all_gather | solution.py:117
  14.1 1049.1 %all-reduce.9.cloned.1.call-start = ((), (), s32[]{:S(2)}) async-start(), calls=%async_computation.4 | async-start | bytes 56623104
  57.9 80.4 %copy-start.36 = (f32[768]{0:T(1024)}, f32[768]{0:T(1024)S(1)}, u32[]{:S(2)}) copy-start(f32[768]{0:T(1024)S(1)} %get-tuple-element.257) | copy-start | bytes 9220
  57.9 80.4 %copy-start.47 = (f32[768]{0:T(1024)}, f32[768]{0:T(1024)S(1)}, u32[]{:S(2)}) copy-start(f32[768]{0:T(1024)S(1)} %get-tuple-element.258) | copy-start | bytes 9220
  60.3 78.0 %copy-start.34 = (f32[1024]{0:T(1024)}, f32[1024]{0:T(1024)S(1)}, u32[]{:S(2)}) copy-start(f32[1024]{0:T(1024)S(1)} %broadcast_multiply_fusion.5) | copy-start | bytes 12292
  60.9 77.4 %copy-start.40 = (f32[1024]{0:T(1024)}, f32[1024]{0:T(1024)S(1)}, u32[]{:S(2)}) copy-start(f32[1024]{0:T(1024)S(1)} %add_rsqrt_fusion) | copy-start | bytes 12292
  62.0 102.1 %copy-start.20 = (f32[1024,16]{0,1:T(8,128)}, f32[1024,16]{0,1:T(8,128)S(1)}, u32[]{:S(2)}) copy-start(f32[1024,16]{0,1:T(8,128)S(1)} %get-tuple-element.253) | copy-start | bytes 196612
  62.1 102.1 %copy-start.23 = (f32[1024,16]{0,1:T(8,128)}, f32[1024,16]{0,1:T(8,128)S(1)}, u32[]{:S(2)}) copy-start(f32[1024,16]{0,1:T(8,128)S(1)} %get-tuple-element.254) | copy-start | bytes 196612
  170.4 23.7 %copy-start.6 = (bf16[1024,12,64]{0,2,1:T(8,128)(2,1)S(1)}, bf16[1024,12,64]{0,2,1:T(8,128)(2,1)}, u32[]{:S(2)}) copy-start(bf16[1024,12,64]{0,2,1:T(8,128)(2,1)} %get-tuple-element.420) | copy-start | bytes 4718596 | tf_op jit(solution)/shard_map/while
  248.9 31.9 %copy-start.2 = (pred[512,1024]{1,0:T(8,128)(4,1)}, pred[512,1024]{1,0:T(8,128)(4,1)S(1)}, u32[]{:S(2)}) copy-start(pred[512,1024]{1,0:T(8,128)(4,1)S(1)} %fusion.148) | copy-start | bytes 1572868 | tf_op jit(solution)/shard_map/while
  370.2 31.5 %copy-start.2 = (pred[512,1024]{1,0:T(8,128)(4,1)}, pred[512,1024]{1,0:T(8,128)(4,1)S(1)}, u32[]{:S(2)}) copy-start(pred[512,1024]{1,0:T(8,128)(4,1)S(1)} %fusion.148) | copy-start | bytes 1572868 | tf_op jit(solution)/shard_map/while
  652.4 44.2 %copy-start.43 = (f32[312]{0:T(512)S(1)}, f32[312]{0:T(512)}, u32[]{:S(2)}) copy-start(f32[312]{0:T(512)} %param.29) | copy-start | bytes 3748
  652.4 44.2 %copy-start.49 = (f32[312]{0:T(512)S(1)}, f32[312]{0:T(512)}, u32[]{:S(2)}) copy-start(f32[312]{0:T(512)} %param.34) | copy-start | bytes 3748
  652.4 44.2 %copy-start.50 = (f32[312]{0:T(512)S(1)}, f32[312]{0:T(512)}, u32[]{:S(2)}) copy-start(f32[312]{0:T(512)} %param.39) | copy-start | bytes 3748
  706.2 357.0 %copy-start.17 = (f32[73728]{0:T(1024)S(1)}, f32[73728]{0:T(1024)}, u32[]{:S(2)}) copy-start(f32[73728]{0:T(1024)} %param.28) | copy-start | bytes 884740
  706.2 357.0 %copy-start.25 = (f32[73728]{0:T(1024)S(1)}, f32[73728]{0:T(1024)}, u32[]{:S(2)}) copy-start(f32[73728]{0:T(1024)} %param.33) | copy-start | bytes 884740
  706.2 357.0 %copy-start.26 = (f32[73728]{0:T(1024)S(1)}, f32[73728]{0:T(1024)}, u32[]{:S(2)}) copy-start(f32[73728]{0:T(1024)} %param.38) | copy-start | bytes 884740
  706.2 359.0 %copy-start.18 = (f32[73728]{0:T(1024)S(1)}, f32[73728]{0:T(1024)}, u32[]{:S(2)}) copy-start(f32[73728]{0:T(1024)} %param.27) | copy-start | bytes 884740
  706.3 359.0 %copy-start.27 = (f32[73728]{0:T(1024)S(1)}, f32[73728]{0:T(1024)}, u32[]{:S(2)}) copy-start(f32[73728]{0:T(1024)} %param.32) | copy-start | bytes 884740
  706.3 359.0 %copy-start.28 = (f32[73728]{0:T(1024)S(1)}, f32[73728]{0:T(1024)}, u32[]{:S(2)}) copy-start(f32[73728]{0:T(1024)} %param.37) | copy-start | bytes 884740
  709.2 358.1 %copy-start.22 = (f32[55296]{0:T(1024)S(1)}, f32[55296]{0:T(1024)}, u32[]{:S(2)}) copy-start(f32[55296]{0:T(1024)} %param.25) | copy-start | bytes 663556
  709.2 358.1 %copy-start.30 = (f32[55296]{0:T(1024)S(1)}, f32[55296]{0:T(1024)}, u32[]{:S(2)}) copy-start(f32[55296]{0:T(1024)} %param.30) | copy-start | bytes 663556
  709.2 358.1 %copy-start.31 = (f32[55296]{0:T(1024)S(1)}, f32[55296]{0:T(1024)}, u32[]{:S(2)}) copy-start(f32[55296]{0:T(1024)} %param.35) | copy-start | bytes 663556
  709.2 360.0 %copy-start.29 = (f32[18432]{0:T(1024)S(1)}, f32[18432]{0:T(1024)}, u32[]{:S(2)}) copy-start(f32[18432]{0:T(1024)} %param.26) | copy-start | bytes 221188
  709.2 360.0 %copy-start.32 = (f32[18432]{0:T(1024)S(1)}, f32[18432]{0:T(1024)}, u32[]{:S(2)}) copy-start(f32[18432]{0:T(1024)} %param.31) | copy-start | bytes 221188
  709.2 360.0 %copy-start.33 = (f32[18432]{0:T(1024)S(1)}, f32[18432]{0:T(1024)}, u32[]{:S(2)}) copy-start(f32[18432]{0:T(1024)} %param.36) | copy-start | bytes 221188
  (35 other events, 276.6 us)
Sparse Core Ops, SparseCore 0:
  11.4 56.8 all-gather.6
  71.7 59.0 all-gather.4
  134.1 62.3 all-gather.8
  199.7 62.3 all-gather.10
  631.0 432.1 all-reduce.8
where the time goes:
time: 1100 us; the launch traced here: 1080 us
  waiting for transfers between devices  415 us (38%)
  matrix products  290 us (26%)
  local copies, waits for them, and re-layouts  159 us (14%)
  other arithmetic  108 us (10%)
  blocking collectives  82.7 us (8%)
  between operations  14.8 us (1%)
    unnamed x6, waiting for transfers between devices  354 us
    unnamed x2, blocking collectives  82.7 us
    dynamic_update_slice x4, local copies, waits for them, and re-layouts, per_device(): context, logsums = lax.map(forward_block, offsets)  63.5 us
    all_gather x1, waiting for transfers between devices, per_device(): lax.all_gather(w_qkv.astype(jnp.bfloat16), ('dp', 'group'), axis=0, tiled...  55 us
    dot_general x4, matrix products, block_scores(): jnp.einsum('qhd,khd->hqk', query_rows, key_rows, preferred_element_type=j...  49.1 us
    convert_element_type x2, other arithmetic, backward_block(): grad_scores = (probs * (dprob - inner)).astype(jnp.bfloat16)  42.4 us
    dot_general x2, matrix products, backward_block(): jnp.einsum('qhd,khd->hqk', upstream, values, preferred_element_type=jnp.f...  36.4 us
    dot_general x1, matrix products, per_device(): jnp.dot(normed_two, weight_up, preferred_element_type=jnp.float32) + bias_up  36.3 us
  transfers between devices with their start and end apart: 5, of which 3 were waited for; matrix products, arithmetic and copies ran while one was open for 44% of the time, Pallas kernels for 0%

commit v1 on v0

v1 whole, which is shorter than its diff:
```python
import jax
import jax.numpy as jnp
from jax import lax
from jax.experimental import pallas as pl
from jax.experimental.pallas import tpu as pltpu
from jax.sharding import PartitionSpec as P

D = 768
HEADS = 12
HEAD = 64
ROT = 16
FF = 3072
TOK_DEV = 1024
BLOCK = 256
PAIR = 2 * HEAD
TRIPLE = 6 * HEAD
STEP = 10


norm_eps = 1e-05
beta_first = 0.9
beta_second = 0.999
learn_rate = 0.05
vector_rate = 0.3
weight_decay = 0.1
adam_eps = 1e-08
masked_value = -1e30
rotary_base = 10000.0


def norm_parts(inputs, gain, shift):
    average = jnp.mean(inputs, axis=-1, keepdims=True)
    centred = inputs - average
    spread = jnp.mean(centred * centred, axis=-1, keepdims=True)
    scaled = lax.rsqrt(spread + norm_eps)
    normal = centred * scaled
    return (normal * gain + shift, normal, scaled)


def norm_back(upstream, normal, scaled, gain):
    weighted = upstream * gain
    inner = weighted - jnp.mean(weighted, axis=-1, keepdims=True)
    inner = inner - normal * jnp.mean(weighted * normal, axis=-1, keepdims=True)
    return (scaled * inner, jnp.sum(upstream * normal, axis=0), jnp.sum(upstream, axis=0))


def packing(lengths):
    seq_ends = jnp.cumsum(lengths)
    row_ids = jnp.arange(TOK_DEV, dtype=jnp.int32)
    passed = row_ids[:, None] >= seq_ends[None, :]
    document = jnp.sum(passed.astype(jnp.int32), axis=1)
    begins = jnp.max(jnp.where(passed, seq_ends[None, :], 0), axis=1)
    return (document, row_ids - begins, row_ids < seq_ends[-1])


def lane_tables(position):
    half_rot = ROT // 2
    inverse = rotary_base ** (-(2.0 * jnp.arange(half_rot, dtype=jnp.float32)) / ROT)
    phases = position.astype(jnp.float32)[:, None] * inverse
    cosines = jnp.cos(phases)
    sines = jnp.sin(phases)
    ones = jnp.ones((TOK_DEV, HEAD - ROT), jnp.float32)
    blank = jnp.zeros((TOK_DEV, HEAD - ROT), jnp.float32)
    gap = jnp.zeros_like(sines)
    keep = jnp.concatenate([cosines, cosines, ones], axis=-1)
    low = jnp.concatenate([-sines, gap, blank], axis=-1)
    high = jnp.concatenate([gap, sines, blank], axis=-1)
    plain = jnp.ones((TOK_DEV, HEAD), jnp.float32)
    empty = jnp.zeros((TOK_DEV, HEAD), jnp.float32)
    return (
        jnp.concatenate([keep, keep, plain] * 2, axis=-1),
        jnp.concatenate([low, low, empty] * 2, axis=-1),
        jnp.concatenate([high, high, empty] * 2, axis=-1),
    )


def dot_nt(left, right):
    return lax.dot_general(
        left, right, (((1,), (1,)), ((), ())), preferred_element_type=jnp.float32
    )


def dot_nn(left, right):
    return lax.dot_general(
        left, right, (((1,), (0,)), ((), ())), preferred_element_type=jnp.float32
    )


def attention_kernel(
    begins_ref,
    normed_ref,
    seed_ref,
    weight_ref,
    bias_ref,
    out_ref,
    keep_ref,
    low_ref,
    high_ref,
    context_ref,
    grad_ref,
    total_ref,
):
    projected = dot_nn(normed_ref[...], weight_ref[...]) + bias_ref[...]
    turned = (
        projected * keep_ref[...]
        + pltpu.roll(projected, TRIPLE - ROT // 2, 1) * low_ref[...]
        + pltpu.roll(projected, ROT // 2, 1) * high_ref[...]
    ).astype(jnp.bfloat16)
    upstream = dot_nt(seed_ref[...], out_ref[...]).astype(jnp.bfloat16)
    scaling = HEAD ** (-0.5)
    heads = []
    for head in range(2):
        at = head * 3 * HEAD
        queries = turned[:, at : at + HEAD] * jnp.bfloat16(scaling)
        keys = turned[:, at + HEAD : at + 2 * HEAD]
        values = turned[:, at + 2 * HEAD : at + 3 * HEAD]
        heads.append(
            (queries, keys, values, upstream[:, head * HEAD : (head + 1) * HEAD], keys.T, values.T)
        )
    total_ref[...] = jnp.zeros_like(total_ref)
    for step in range(TOK_DEV // BLOCK):
        first, last = step * BLOCK, (step + 1) * BLOCK
        begins = begins_ref[:, first:last]
        key_ids = lax.broadcasted_iota(jnp.int32, (last, BLOCK), 0)
        query_ids = first + lax.broadcasted_iota(jnp.int32, (last, BLOCK), 1)
        allowed = (key_ids >= begins) & (key_ids <= query_ids)
        contexts = []
        for head in range(2):
            at = head * 3 * HEAD
            queries, keys, values, above, keys_t, values_t = heads[head]
            query_rows = queries[first:last]
            above_rows = above[first:last]
            scores = jnp.where(allowed, dot_nt(keys[:last], query_rows), masked_value)
            highest = jnp.max(scores, axis=0, keepdims=True)
            expanded = jnp.exp(scores - highest)
            inverse = 1.0 / jnp.sum(expanded, axis=0, keepdims=True)
            probs = expanded * inverse
            probs_low = probs.astype(jnp.bfloat16)
            contexts.append(dot_nn(values_t[:, :last], probs_low))
            dprob = dot_nt(values[:last], above_rows)
            inner = jnp.sum(probs * dprob, axis=0, keepdims=True)
            grad_scores = (probs * (dprob - inner)).astype(jnp.bfloat16)
            grad_queries = dot_nn(keys_t[:, :last], grad_scores) * scaling
            total_ref[first:last, at : at + HEAD] = grad_queries.T
            total_ref[:last, at + HEAD : at + 2 * HEAD] += dot_nn(grad_scores, query_rows)
            total_ref[:last, at + 2 * HEAD : at + 3 * HEAD] += dot_nn(probs_low, above_rows)
        context_ref[first:last, :] = jnp.concatenate(contexts, axis=0).T.astype(jnp.bfloat16)
    total = total_ref[...]
    grad_ref[...] = (
        total * keep_ref[...]
        - pltpu.roll(total, TRIPLE - ROT // 2, 1) * low_ref[...]
        - pltpu.roll(total, ROT // 2, 1) * high_ref[...]
    ).astype(jnp.bfloat16)


def attention(begins, normed, seed_rows, weight_qkv, bias_qkv, weight_out, tables):
    whole = lambda rows, columns: pl.BlockSpec((rows, columns), lambda j: (0, 0))
    pairs = HEADS // 2
    return pl.pallas_call(
        attention_kernel,
        grid=(pairs,),
        in_specs=[
            whole(1, TOK_DEV),
            whole(TOK_DEV, D),
            whole(TOK_DEV, D),
            pl.BlockSpec((D, TRIPLE), lambda j: (0, j)),
            pl.BlockSpec((1, TRIPLE), lambda j: (0, j)),
            pl.BlockSpec((PAIR, D), lambda j: (j, 0)),
            whole(TOK_DEV, TRIPLE),
            whole(TOK_DEV, TRIPLE),
            whole(TOK_DEV, TRIPLE),
        ],
        out_specs=[
            pl.BlockSpec((TOK_DEV, PAIR), lambda j: (0, j)),
            pl.BlockSpec((TOK_DEV, TRIPLE), lambda j: (0, j)),
        ],
        out_shape=[
            jax.ShapeDtypeStruct((TOK_DEV, D), jnp.bfloat16),
            jax.ShapeDtypeStruct((TOK_DEV, 3 * D), jnp.bfloat16),
        ],
        scratch_shapes=[pltpu.VMEM((TOK_DEV, TRIPLE), jnp.float32)],
        compiler_params=pltpu.CompilerParams(vmem_limit_bytes=52 * 2**20),
        cost_estimate=pl.CostEstimate(
            flops=16_000_000_000, bytes_accessed=20_000_000, transcendentals=8_000_000
        ),
    )(begins, normed, seed_rows, weight_qkv, bias_qkv, weight_out, *tables)


def adam_step(weight, gradient, moment_one, moment_two, decay_rate, step_rate):
    moment_one = beta_first * moment_one + (1.0 - beta_first) * gradient
    moment_two = beta_second * moment_two + (1.0 - beta_second) * gradient * gradient
    first_hat = moment_one / (1.0 - beta_first**STEP)
    second_hat = moment_two / (1.0 - beta_second**STEP)
    weight = weight - step_rate * (
        first_hat / (jnp.sqrt(second_hat) + adam_eps) + decay_rate * weight
    )
    return (weight, moment_one, moment_two)


def per_device(
    tokens,
    cotangent,
    seq_lens,
    w_qkv,
    w_out,
    w_up,
    w_down,
    vectors,
    first_qkv,
    first_out,
    first_up,
    first_down,
    first_vec,
    second_qkv,
    second_out,
    second_up,
    second_down,
    second_vec,
):
    axes = ("dp", "group")
    shards = D // (w_out.shape[0] // D)

    def gather(shard, rows):
        low = shard.astype(jnp.bfloat16).reshape(rows // shards, -1)
        return lax.all_gather(low, axes, axis=0, tiled=True)

    weight_qkv = gather(w_qkv, D)
    weight_out = gather(w_out, D)
    weight_up = gather(w_up, D)
    weight_down = gather(w_down, FF)
    packed = lax.all_gather(vectors.astype(jnp.bfloat16), axes, axis=0, tiled=True).astype(jnp.float32)
    gain_one = packed[0:D]
    gain_two = packed[D : 2 * D]
    shift_one = packed[2 * D : 3 * D]
    shift_two = packed[3 * D : 4 * D]
    bias_qkv = packed[4 * D : 7 * D]
    bias_out = packed[7 * D : 8 * D]
    bias_up = packed[8 * D : 8 * D + FF]
    bias_down = packed[8 * D + FF :]
    document, position, live_rows = packing(seq_lens[0])
    inputs = tokens.astype(jnp.float32)
    normed_one, normal_one, scaled_one = norm_parts(inputs, gain_one, shift_one)
    normed_two, normal_two, scaled_two = norm_parts(inputs, gain_two, shift_two)
    normed_one = normed_one.astype(jnp.bfloat16)
    normed_two = normed_two.astype(jnp.bfloat16)
    seed_rows = jnp.where(live_rows[:, None], cotangent, jnp.zeros_like(cotangent))
    begins = jnp.arange(TOK_DEV, dtype=jnp.int32) - position
    context, grad_projected = attention(
        begins[None, :],
        normed_one,
        seed_rows,
        weight_qkv,
        bias_qkv[None, :],
        weight_out,
        lane_tables(position),
    )
    attended = jnp.dot(context, weight_out, preferred_element_type=jnp.float32) + bias_out
    hidden = jnp.dot(normed_two, weight_up, preferred_element_type=jnp.float32) + bias_up
    activation, gelu_back = jax.vjp(lambda entry: jax.nn.gelu(entry, approximate=False), hidden)
    activated = activation.astype(jnp.bfloat16)
    result = (
        inputs
        + attended
        + jnp.dot(activated, weight_down, preferred_element_type=jnp.float32)
        + bias_down
    )
    seed_float = seed_rows.astype(jnp.float32)
    grad_down = jnp.einsum("tf,td->fd", activated, seed_rows, preferred_element_type=jnp.float32)
    grad_out = jnp.einsum("tc,td->cd", context, seed_rows, preferred_element_type=jnp.float32)
    grad_act = jnp.einsum("td,fd->tf", seed_rows, weight_down, preferred_element_type=jnp.float32)
    grad_hidden = gelu_back(grad_act)[0].astype(jnp.bfloat16)
    grad_up = jnp.einsum("td,tf->df", normed_two, grad_hidden, preferred_element_type=jnp.float32)
    grad_two = jnp.einsum("tf,df->td", grad_hidden, weight_up, preferred_element_type=jnp.float32)
    grad_qkv = jnp.einsum(
        "td,te->de", normed_one, grad_projected, preferred_element_type=jnp.float32
    )
    grad_one = jnp.einsum(
        "te,de->td", grad_projected, weight_qkv, preferred_element_type=jnp.float32
    )
    input_one, gain_grad_one, shift_grad_one = norm_back(grad_one, normal_one, scaled_one, gain_one)
    input_two, gain_grad_two, shift_grad_two = norm_back(grad_two, normal_two, scaled_two, gain_two)
    input_grad = seed_float + input_one + input_two
    seed_total = jnp.sum(seed_float, axis=0)
    grad_vec = jnp.concatenate(
        [
            gain_grad_one,
            gain_grad_two,
            shift_grad_one,
            shift_grad_two,
            jnp.sum(grad_projected.astype(jnp.float32), axis=0),
            seed_total,
            jnp.sum(grad_hidden.astype(jnp.float32), axis=0),
            seed_total,
        ]
    )
    def scatter(gradient):
        low = gradient.astype(jnp.bfloat16)
        part = lax.psum_scatter(low, axes, scatter_dimension=0, tiled=True)
        return part.astype(jnp.float32).reshape(-1)

    summed = (
        scatter(grad_qkv),
        scatter(grad_out),
        scatter(grad_up),
        scatter(grad_down),
        lax.psum_scatter(grad_vec, axes, scatter_dimension=0, tiled=True),
    )
    masters = (w_qkv, w_out, w_up, w_down, vectors)
    firsts = (first_qkv, first_out, first_up, first_down, first_vec)
    seconds = (second_qkv, second_out, second_up, second_down, second_vec)
    decays = (weight_decay, weight_decay, weight_decay, weight_decay, 0.0)
    rates = (learn_rate, learn_rate, learn_rate, learn_rate, vector_rate)
    updated = [
        adam_step(weight, gradient, moment_one, moment_two, decay_rate, step_rate)
        for weight, gradient, moment_one, moment_two, decay_rate, step_rate in zip(
            masters, summed, firsts, seconds, decays, rates
        )
    ]
    return (
        result.astype(jnp.bfloat16),
        input_grad,
        updated[0][0],
        updated[1][0],
        updated[2][0],
        updated[3][0],
        updated[4][0],
        updated[0][1],
        updated[1][1],
        updated[2][1],
        updated[3][1],
        updated[4][1],
        updated[0][2],
        updated[1][2],
        updated[2][2],
        updated[3][2],
        updated[4][2],
    )


def solution(mesh):
    placed = (
        P(("dp", "group"), None),
        P(("dp", "group"), None),
        P(("dp", "group"), None),
        P(("dp", "group")),
        P(("dp", "group")),
        P(("dp", "group")),
        P(("dp", "group")),
        P(("dp", "group")),
        P(("dp", "group")),
        P(("dp", "group")),
        P(("dp", "group")),
        P(("dp", "group")),
        P(("dp", "group")),
        P(("dp", "group")),
        P(("dp", "group")),
        P(("dp", "group")),
        P(("dp", "group")),
        P(("dp", "group")),
    )
    return jax.shard_map(
        per_device,
        mesh=mesh,
        in_specs=placed,
        out_specs=(
            P(("dp", "group"), None),
            P(("dp", "group"), None),
            P(("dp", "group")),
            P(("dp", "group")),
            P(("dp", "group")),
            P(("dp", "group")),
            P(("dp", "group")),
            P(("dp", "group")),
            P(("dp", "group")),
            P(("dp", "group")),
            P(("dp", "group")),
            P(("dp", "group")),
            P(("dp", "group")),
            P(("dp", "group")),
            P(("dp", "group")),
            P(("dp", "group")),
            P(("dp", "group")),
        ),
        check_vma=False,
    )
```

time: 1100 us -> 736 us (0.67); the launches traced: 1080 us -> 727 us
  matrix products: 290 us -> 113 us
  local copies, waits for them, and re-layouts: 159 us -> 33 us
  Pallas kernels: 0 us -> 77.2 us
  other arithmetic: 108 us -> 31.7 us
  waiting for transfers between devices: 415 us -> 373 us
    unnamed x6 -> x8, waiting for transfers between devices: 354 us -> 0.13 us
    reduce_scatter x0 -> x4, waiting for transfers between devices: none -> 250 us  [scatter(): part = lax.psum_scatter(low, axes, scatter_dimension=0, tiled=True)]
    dot_general x16 -> x0, matrix products: 182 us -> none  [the longest x4 49.1 us: block_scores(): jnp.einsum('qhd,khd->hqk', query_rows, key_rows, preferred_element_type=j...]
    pallas_call x0 -> x1, Pallas kernels: none -> 77.2 us  [attention(): pl.pallas_call(attention_kernel, grid=(pairs,), in_specs=[whole(1, TOK_DE...]
    dynamic_update_slice x4 -> x0, local copies, waits for them, and re-layouts: 63.5 us -> none  [per_device(): context, logsums = lax.map(forward_block, offsets)]
    all_gather x4, waiting for transfers between devices: 60.6 us -> 123 us  [gather(): return lax.all_gather(low, axes, axis=0, tiled=True)]
    reshape x8 -> x7, local copies, waits for them, and re-layouts: 56.1 us -> 6.81 us  [the longest x4 3.91 us: gather(): low = shard.astype(jnp.bfloat16).reshape(rows // shards, -1)]
    convert_element_type x7 -> x5, other arithmetic: 49 us -> 4.71 us  [the longest x3 2.93 us: gather(): low = shard.astype(jnp.bfloat16).reshape(rows // shards, -1)]
  transfers between devices with their start and end apart: 5 -> 8, of which waited for: 3 -> 7; matrix products, arithmetic and copies ran while one was open for 44% -> 20% of each run, Pallas kernels for 0% -> 11%
where the time goes in v1:
time: 736 us; the launch traced here: 727 us
  waiting for transfers between devices  373 us (51%)
  matrix products  113 us (15%)
  blocking collectives  82.9 us (11%)
  Pallas kernels  77.2 us (10%)
  local copies, waits for them, and re-layouts  33 us (4%)
  other arithmetic  31.7 us (4%)
  between operations  14.8 us (2%)
    reduce_scatter x4, waiting for transfers between devices, scatter(): part = lax.psum_scatter(low, axes, scatter_dimension=0, tiled=True)  250 us
    all_gather x4, waiting for transfers between devices, gather(): return lax.all_gather(low, axes, axis=0, tiled=True)  123 us
    unnamed x2, blocking collectives  82.9 us
    pallas_call x1, Pallas kernels, attention(): pl.pallas_call(attention_kernel, grid=(pairs,), in_specs=[whole(1, TOK_DE...  77.2 us
    dot_general x1, matrix products, per_device(): jnp.dot(normed_two, weight_up, preferred_element_type=jnp.float32) + bias_up  37.4 us
    dot_general x1, matrix products, per_device(): jnp.einsum('td,fd->tf', seed_rows, weight_down, preferred_element_type=jn...  16.7 us
  transfers between devices with their start and end apart: 8, of which 7 were waited for; matrix products, arithmetic and copies ran while one was open for 20% of the time, Pallas kernels for 11%

profile of v1, /device:TPU:0, one launch (start us, length us, event | category | flops | bytes accessed | tf_op | source)
XLA Modules:
  0.0 726.8 jit_solution(17561743873738825136)
XLA Ops:
  13.5 42.5 %all-reduce = bf16[9984]{0:T(1024)(128)(2,1)S(1)} all-reduce(bf16[9984]{0:T(1024)(128)(2,1)S(1)} %dynamic-update-slice), channel_id=1, replica_groups=mesh['dp'=8,'group'=4] {'dp','group'}, use_global_device_ids=true, to_apply=%add | all-reduce | flops 9984 | bytes 39936
  58.3 2.0 fusion.29
  61.7 2.4 convert_reduce_fusion.3
  64.2 13.6 %all-gather.9.cloned.1.call-done = bf16[768,3072]{1,0:T(8,128)(2,1)} async-done(((bf16[24,3072]{1,0:T(8,128)(2,1)}), bf16[768,3072]{1,0:T(8,128)(2,1)}) %all-gather.9.cloned.1.call-update) | async-done | bytes 4718608 | tf_op jit(solution)/shard_map/all_gather | solution.py:225
  77.8 37.4 %multiply_convert_fusion = (bf16[1024,3072]{1,0:T(8,128)(2,1)S(1)}, f32[1024,3072]{1,0:T(8,128)}, f32[1024,3072]{1,0:T(8,128)}) fusion(f32[3072]{0:T(1024)S(1)} %slice.43, bf16[768,3072]{1,0:T(8,128)(2,1)} %all-gather.9.cloned.1.call-done, bf16[1024,768]{1,0:T(8,128)(2,1)S(1)} %copy-done.2, f32[768]{0:T(1024)S(1)} %get-tuple-element.58, ...), kind=kOutput, calls=%fused_computation.4 | convolution fusion | flops 5044174848 | bytes 37775360 | tf_op jit(solution)/shard_map/dot_general | solution.py:258
  115.1 2.6 copy-done.21
  117.8 7.3 %convolution_convert_fusion = bf16[3072,768]{1,0:T(8,128)(2,1)} fusion(bf16[1024,3072]{1,0:T(8,128)(2,1)S(1)} %get-tuple-element.50, bf16[1024,768]{1,0:T(8,128)(2,1)S(1)} %get-tuple-element.37.seed_ref), kind=kOutput, calls=%fused_computation.19 | convolution fusion | flops 4834197504 | bytes 12582912 | tf_op jit(solution)/shard_map/tf,td->fd/dot_general | solution.py:268
  125.3 3.1 multiply_sine_fusion
  129.3 6.4 concatenate.19.low_ref
  135.7 6.7 concatenate.20.high_ref
  142.4 6.0 concatenate.18.keep_ref
  150.2 46.5 %all-gather.5.cloned.1.call-done.weight_ref = bf16[768,2304]{1,0:T(8,128)(2,1)} async-done(((bf16[24,2304]{1,0:T(8,128)(2,1)}), bf16[768,2304]{1,0:T(8,128)(2,1)}) %all-gather.5.cloned.1.call-update) | async-done | bytes 3538960 | tf_op jit(solution)/shard_map/all_gather | solution.py:225
  197.9 77.2 %shard_map.305 = (bf16[1024,768]{1,0:T(8,128)(2,1)}, bf16[1024,2304]{1,0:T(8,128)(2,1)}) custom-call(s32[1,1024]{1,0:T(1,128)S(1)} %subtract_subtract_fusion.begins_ref, bf16[1024,768]{1,0:T(8,128)(2,1)} %fusion.17.normed_ref, bf16[1024,768]{1,0:T(8,128)(2,1)} %copy-done.3, bf16[768,2304]{1,0:T(8,128)(2,1)} %all-gather.5.cloned.1.call-done.weight_ref, ...), custom_call_target="tpu_custom_call" | custom-call | flops 16000000000 | bytes 20000000 | tf_op jit(solution)/shard_map/pallas_call | solution.py:159
  275.1 4.0 convolution_convert_fusion.3
  279.1 7.9 %convolution_convert_fusion.2 = bf16[768,2304]{1,0:T(8,128)(2,1)} fusion(bf16[1024,768]{1,0:T(8,128)(2,1)S(1)} %copy-done.9, bf16[1024,2304]{1,0:T(8,128)(2,1)} %get-tuple-element.20), kind=kOutput, calls=%fused_computation.21 | convolution fusion | flops 3625648128 | bytes 9830400 | tf_op jit(solution)/shard_map/td,te->de/dot_general | solution.py:274
  287.1 20.7 %reduce-scatter.11.cloned.1.call-done = bf16[96,768]{1,0:T(8,128)(2,1)} async-done(((bf16[3072,768]{1,0:T(8,128)(2,1)}), bf16[96,768]{1,0:T(8,128)(2,1)}) %reduce-scatter.11.cloned.1.call-update) | async-done | bytes 147472 | tf_op jit(solution)/shard_map/reduce_scatter | solution.py:298
  308.8 2.4 multiply_subtract_fusion
  313.1 3.0 convert_reduce_fusion.1
  316.1 92.7 %reduce-scatter.7.cloned.1.call-done = bf16[24,768]{1,0:T(8,128)(2,1)} async-done(((bf16[768,768]{1,0:T(8,128)(2,1)}), bf16[24,768]{1,0:T(8,128)(2,1)}) %reduce-scatter.7.cloned.1.call-update) | async-done | bytes 36880 | tf_op jit(solution)/shard_map/reduce_scatter | solution.py:298
  411.3 105.9 %reduce-scatter.5.cloned.1.call-done = bf16[24,2304]{1,0:T(8,128)(2,1)} async-done(((bf16[768,2304]{1,0:T(8,128)(2,1)}), bf16[24,2304]{1,0:T(8,128)(2,1)}) %reduce-scatter.5.cloned.1.call-update) | async-done | bytes 110608 | tf_op jit(solution)/shard_map/reduce_scatter | solution.py:298
  518.2 2.1 multiply_subtract_fusion.2
  520.3 63.2 %all-gather.11.cloned.1.call-done = bf16[3072,768]{1,0:T(8,128)(2,1)} async-done(((bf16[96,768]{1,0:T(8,128)(2,1)}), bf16[3072,768]{1,0:T(8,128)(2,1)}) %all-gather.11.cloned.1.call-update) | async-done | bytes 4718608 | tf_op jit(solution)/shard_map/all_gather | solution.py:225
  583.5 16.7 %convert_reduce_fusion = (f32[3072]{0:T(1024)S(1)}, bf16[1024,3072]{1,0:T(8,128)(2,1)}) fusion(f32[1024,3072]{1,0:T(8,128)} %get-tuple-element.51, bf16[1024,768]{1,0:T(8,128)(2,1)S(1)} %copy-done.5, bf16[3072,768]{1,0:T(8,128)(2,1)} %all-gather.11.cloned.1.call-done, f32[1024,3072]{1,0:T(8,128)} %get-tuple-element.62, f32[3072]{0:T(1024)S(1)} %slice.43), kind=kOutput, calls=%fused_computation.2 | convolution fusion | flops 4885312512 | bytes 37773312 | tf_op jit(solution)/shard_map/td,fd->tf/dot_general | solution.py:270
  600.2 9.9 %convolution_convert_fusion.1 = bf16[768,3072]{1,0:T(8,128)(2,1)} fusion(bf16[1024,3072]{1,0:T(8,128)(2,1)} %get-tuple-element.65, bf16[1024,768]{1,0:T(8,128)(2,1)S(1)} %copy-done.2, f32[768]{0:T(1024)S(1)} %get-tuple-element.58, f32[768]{0:T(1024)S(1)} %get-tuple-element.57, f32[1024]{0:T(1024)S(1)} %add_rsqrt_fusion, f32[1024]{0:T(1024)S(1)} %broadcast_multiply_fusion.4), kind=kOutput, calls=%fused_computation.20 | convolution fusion | flops 4838916096 | bytes 12597248 | tf_op jit(solution)/shard_map/td,tf->df/dot_general | solution.py:272
  610.1 8.7 %fusion.50 = f32[1024,768]{1,0:T(8,128)S(1)} fusion(bf16[1024,3072]{1,0:T(8,128)(2,1)} %get-tuple-element.65, bf16[768,3072]{1,0:T(8,128)(2,1)} %all-gather.9.cloned.1.call-done), kind=kOutput, calls=%fused_computation.105 | convolution fusion | flops 4831838208 | bytes 14155776 | tf_op jit(solution)/shard_map/tf,df->td/dot_general | solution.py:273
  618.9 10.0 %fusion.27 = (f32[768]{0:T(1024)S(1)}, f32[1024]{0:T(1024)S(1)}, f32[1024]{0:T(1024)S(1)}, f32[768]{0:T(1024)S(1)}, f32[768]{0:T(1024)S(1)}, /*index=5*/f32[1024...) fusion(bf16[1024,768]{1,0:T(8,128)(2,1)S(1)} %copy-done.2, f32[1024]{0:T(1024)S(1)} %add_rsqrt_fusion, ...), kind=kOutput, calls=%fused_computation.48 | convolution fusion | flops 3637240832 | bytes 16164864 | tf_op jit(solution)/shard_map/te,de->td/dot_general | solution.py:277
  629.0 40.4 %all-reduce.1 = f32[9984]{0:T(1024)S(1)} all-reduce(f32[9984]{0:T(1024)S(1)} %constant_dynamic-update-slice_fusion), channel_id=6, replica_groups=mesh['dp'=8,'group'=4] {'dp','group'}, use_global_device_ids=true, to_apply=%region_19.20.clone | all-reduce | flops 9984 | bytes 79872
  670.1 8.9 %fusion.49 = f32[1024,768]{1,0:T(8,128)S(1)} fusion(bf16[1024,3072]{1,0:T(8,128)(2,1)} %copy-done.21, bf16[3072,768]{1,0:T(8,128)(2,1)} %all-gather.11.cloned.1.call-done), kind=kOutput, calls=%fused_computation.104 | convolution fusion | flops 4831838208 | bytes 14155776 | tf_op jit(solution)/shard_map/dot_general | solution.py:264
  679.1 2.6 fusion.32
  682.5 3.3 fusion.26
  685.8 30.8 %reduce-scatter.9.cloned.1.call-done = bf16[24,3072]{1,0:T(8,128)(2,1)} async-done(((bf16[768,3072]{1,0:T(8,128)(2,1)}), bf16[24,3072]{1,0:T(8,128)(2,1)}) %reduce-scatter.9.cloned.1.call-update) | async-done | bytes 147472 | tf_op jit(solution)/shard_map/reduce_scatter | solution.py:298
  717.6 2.1 multiply_subtract_fusion.1
  (108 shorter events, 23.1 us)
Async XLA Ops:
  7.2 70.6 %copy-start.2 = (bf16[1024,768]{1,0:T(8,128)(2,1)S(1)}, bf16[1024,768]{1,0:T(8,128)(2,1)}, u32[]{:S(2)}) copy-start(bf16[1024,768]{1,0:T(8,128)(2,1)} %param.18) | copy-start | bytes 4718596
  7.2 53.1 %copy-start.19 = (s32[1,4]{1,0:T(1,128)S(1)}, s32[1,4]{1,0:T(1,128)}, u32[]{:S(2)}) copy-start(s32[1,4]{1,0:T(1,128)} %param.20) | copy-start | bytes 52
  7.2 70.5 %all-gather.9.cloned.1.call-start = ((), (), s32[]{:S(2)}) async-start(), calls=%async_computation.6 | async-start | bytes 4866048 | tf_op jit(solution)/shard_map/all_gather | solution.py:225
  9.1 141.1 %all-gather.7.cloned.1.call-start = ((), (), s32[]{:S(2)}) async-start(), calls=%async_computation.5 | async-start | bytes 1216512 | tf_op jit(solution)/shard_map/all_gather | solution.py:225
  10.7 185.9 %all-gather.5.cloned.1.call-start = ((), (), s32[]{:S(2)}) async-start(), calls=%async_computation.4 | async-start | bytes 3649536 | tf_op jit(solution)/shard_map/all_gather | solution.py:225
  12.6 295.2 %reduce-scatter.11.cloned.1.call-start = ((), (), s32[]{:S(2)}) async-start(), calls=%async_computation.11 | async-start | bytes 4866048 | tf_op jit(solution)/shard_map/reduce_scatter | solution.py:298
  64.2 51.0 %copy-start.3 = (bf16[1024,768]{1,0:T(8,128)(2,1)}, bf16[1024,768]{1,0:T(8,128)(2,1)S(1)}, u32[]{:S(2)}) copy-start(bf16[1024,768]{1,0:T(8,128)(2,1)S(1)} %get-tuple-element.37.seed_ref) | copy-start | bytes 4718596
  115.1 2.6 copy-start.21
  125.1 283.7 %reduce-scatter.7.cloned.1.call-start = ((), (), s32[]{:S(2)}) async-start(), calls=%async_computation.9 | async-start | bytes 1216512 | tf_op jit(solution)/shard_map/reduce_scatter | solution.py:298
  196.6 1.3 copy-start
  197.9 77.2 %copy-start.4 = (bf16[1024,768]{1,0:T(8,128)(2,1)S(1)}, bf16[1024,768]{1,0:T(8,128)(2,1)}, u32[]{:S(2)}) copy-start(bf16[1024,768]{1,0:T(8,128)(2,1)} %copy-done.3) | copy-start | bytes 4718596
  275.1 4.1 copy-start.9
  279.1 238.1 %reduce-scatter.5.cloned.1.call-start = ((), (), s32[]{:S(2)}) async-start(), calls=%async_computation.8 | async-start | bytes 3649536 | tf_op jit(solution)/shard_map/reduce_scatter | solution.py:298
  287.0 122.6 %copy-start.11 = (f32[18432]{0:T(1024)S(1)}, f32[18432]{0:T(1024)}, u32[]{:S(2)}) copy-start(f32[18432]{0:T(1024)} %param.22) | copy-start | bytes 221188
  287.0 296.4 %all-gather.11.cloned.1.call-start = ((), (), s32[]{:S(2)}) async-start(), calls=%async_computation.7 | async-start | bytes 4866048 | tf_op jit(solution)/shard_map/all_gather | solution.py:225
  308.8 274.7 %copy-start.5 = (bf16[1024,768]{1,0:T(8,128)(2,1)S(1)}, bf16[1024,768]{1,0:T(8,128)(2,1)}, u32[]{:S(2)}) copy-start(bf16[1024,768]{1,0:T(8,128)(2,1)} %copy-done.3) | copy-start | bytes 4718596
  313.0 403.6 %reduce-scatter.9.cloned.1.call-start = ((), (), s32[]{:S(2)}) async-start(), calls=%async_computation.10 | async-start | bytes 4866048 | tf_op jit(solution)/shard_map/reduce_scatter | solution.py:298
  610.1 8.8 %copy-start.18 = (bf16[768,2304]{1,0:T(8,128)(2,1)S(1)}, bf16[768,2304]{1,0:T(8,128)(2,1)}, u32[]{:S(2)}) copy-start(bf16[768,2304]{1,0:T(8,128)(2,1)} %all-gather.5.cloned.1.call-done.weight_ref) | copy-start | bytes 10616836
  618.8 10.0 %copy-start.6 = (f32[1024,768]{1,0:T(8,128)}, f32[1024,768]{1,0:T(8,128)S(1)}, u32[]{:S(2)}) copy-start(f32[1024,768]{1,0:T(8,128)S(1)} %fusion.50) | copy-start | bytes 9437188
  618.8 10.1 %copy-start.12 = (f32[768]{0:T(1024)S(1)}, f32[768]{0:T(1024)}, u32[]{:S(2)}) copy-start(f32[768]{0:T(1024)} %get-tuple-element.36) | copy-start | bytes 9220
  618.9 50.5 %copy-start.13 = (f32[312]{0:T(512)S(1)}, f32[312]{0:T(512)}, u32[]{:S(2)}) copy-start(f32[312]{0:T(512)} %param.25) | copy-start | bytes 3748
  618.9 50.5 %copy-start.16 = (f32[312]{0:T(512)S(1)}, f32[312]{0:T(512)}, u32[]{:S(2)}) copy-start(f32[312]{0:T(512)} %param.30) | copy-start | bytes 3748
  618.9 50.5 %copy-start.17 = (f32[312]{0:T(512)S(1)}, f32[312]{0:T(512)}, u32[]{:S(2)}) copy-start(f32[312]{0:T(512)} %param.35) | copy-start | bytes 3748
  670.1 9.0 %copy-start.1 = (bf16[768,768]{1,0:T(8,128)(2,1)S(1)}, bf16[768,768]{1,0:T(8,128)(2,1)}, u32[]{:S(2)}) copy-start(bf16[768,768]{1,0:T(8,128)(2,1)} %all-gather.7.cloned.1.call-done.out_ref) | copy-start | bytes 3538948
  670.1 9.0 %copy-start.14 = (f32[768]{0:T(1024)S(1)}, f32[768]{0:T(1024)}, u32[]{:S(2)}) copy-start(f32[768]{0:T(1024)} %get-tuple-element.53) | copy-start | bytes 9220
  670.1 9.0 %copy-start.15 = (f32[768]{0:T(1024)S(1)}, f32[768]{0:T(1024)}, u32[]{:S(2)}) copy-start(f32[768]{0:T(1024)} %get-tuple-element.54) | copy-start | bytes 9220
  670.1 9.0 %copy-start.20 = (bf16[1024,768]{1,0:T(8,128)(2,1)S(1)}, bf16[1024,768]{1,0:T(8,128)(2,1)}, u32[]{:S(2)}) copy-start(bf16[1024,768]{1,0:T(8,128)(2,1)} %get-tuple-element.19) | copy-start | bytes 4718596
  679.1 2.7 copy-start.7
  679.1 3.4 copy-start.8
  682.5 35.1 %copy-start.10 = (f32[73728]{0:T(1024)S(1)}, f32[73728]{0:T(1024)}, u32[]{:S(2)}) copy-start(f32[73728]{0:T(1024)} %param.23) | copy-start | bytes 884740
Sparse Core Ops, SparseCore 0:
  11.4 66.2 all-gather.8
  81.1 52.9 all-gather.6
  137.5 59.0 all-gather.4
  202.0 105.7 reduce-scatter.10
  313.5 95.2 reduce-scatter.6
  415.0 102.1 reduce-scatter.4
  520.9 62.5 all-gather.10
  610.2 106.3 reduce-scatter.8

commit v2 on v1

--- a/solution.py
+++ b/solution.py
@@ -1,3 +1,5 @@
+import functools
+
 import jax
 import jax.numpy as jnp
 from jax import lax
@@ -62,16 +64,18 @@
     ones = jnp.ones((TOK_DEV, HEAD - ROT), jnp.float32)
     blank = jnp.zeros((TOK_DEV, HEAD - ROT), jnp.float32)
     gap = jnp.zeros_like(sines)
-    keep = jnp.concatenate([cosines, cosines, ones], axis=-1)
-    low = jnp.concatenate([-sines, gap, blank], axis=-1)
-    high = jnp.concatenate([gap, sines, blank], axis=-1)
-    plain = jnp.ones((TOK_DEV, HEAD), jnp.float32)
-    empty = jnp.zeros((TOK_DEV, HEAD), jnp.float32)
     return (
-        jnp.concatenate([keep, keep, plain] * 2, axis=-1),
-        jnp.concatenate([low, low, empty] * 2, axis=-1),
-        jnp.concatenate([high, high, empty] * 2, axis=-1),
-    )
+        jnp.concatenate([cosines, cosines, ones] * 2, axis=-1),
+        jnp.concatenate([-sines, gap, blank] * 2, axis=-1),
+        jnp.concatenate([gap, sines, blank] * 2, axis=-1),
+    )
+
+
+def widen(narrow, plain):
+    lane = lax.broadcasted_iota(jnp.int32, narrow.shape, 1)
+    upper = jnp.where(lane >= HEAD, narrow, plain)
+    lower = jnp.where(lane < HEAD, narrow, plain)
+    return jnp.concatenate([narrow, upper, lower], axis=1)
 
 
 def dot_nt(left, right):
@@ -93,13 +97,22 @@
     weight_ref,
     bias_ref,
     out_ref,
+    cosines_ref,
+    low_sines_ref,
+    high_sines_ref,
+    context_ref,
+    grad_ref,
+    total_ref,
     keep_ref,
     low_ref,
     high_ref,
-    context_ref,
-    grad_ref,
-    total_ref,
 ):
+    @pl.when(pl.program_id(0) == 0)
+    def _():
+        keep_ref[...] = widen(cosines_ref[...], 1.0)
+        low_ref[...] = widen(low_sines_ref[...], 0.0)
+        high_ref[...] = widen(high_sines_ref[...], 0.0)
+
     projected = dot_nn(normed_ref[...], weight_ref[...]) + bias_ref[...]
     turned = (
         projected * keep_ref[...]
@@ -166,9 +179,9 @@
             pl.BlockSpec((D, TRIPLE), lambda j: (0, j)),
             pl.BlockSpec((1, TRIPLE), lambda j: (0, j)),
             pl.BlockSpec((PAIR, D), lambda j: (j, 0)),
-            whole(TOK_DEV, TRIPLE),
-            whole(TOK_DEV, TRIPLE),
-            whole(TOK_DEV, TRIPLE),
+            whole(TOK_DEV, PAIR),
+            whole(TOK_DEV, PAIR),
+            whole(TOK_DEV, PAIR),
         ],
         out_specs=[
             pl.BlockSpec((TOK_DEV, PAIR), lambda j: (0, j)),
@@ -178,12 +191,63 @@
             jax.ShapeDtypeStruct((TOK_DEV, D), jnp.bfloat16),
             jax.ShapeDtypeStruct((TOK_DEV, 3 * D), jnp.bfloat16),
         ],
-        scratch_shapes=[pltpu.VMEM((TOK_DEV, TRIPLE), jnp.float32)],
+        scratch_shapes=[pltpu.VMEM((TOK_DEV, TRIPLE), jnp.float32)] * 4,
         compiler_params=pltpu.CompilerParams(vmem_limit_bytes=52 * 2**20),
         cost_estimate=pl.CostEstimate(
             flops=16_000_000_000, bytes_accessed=20_000_000, transcendentals=8_000_000
         ),
     )(begins, normed, seed_rows, weight_qkv, bias_qkv, weight_out, *tables)
+
+
+def exchange(block, bit, devices):
+    pairs = [(index, index ^ (1 << bit)) for index in range(devices)]
+    return lax.ppermute(block, ("dp", "group"), pairs)
+
+
+def own_bit(bit, group_size):
+    index = lax.axis_index("dp") * group_size + lax.axis_index("group")
+    return lax.rem(lax.div(index, 1 << bit), 2)
+
+
+def bit_order(devices, group_size, flipped):
+    group_bits = group_size.bit_length() - 1
+    total_bits = devices.bit_length() - 1
+    chips = list(range(group_bits + 1, total_bits))
+    if flipped:
+        chips = chips[::-1]
+    return [group_bits] + chips + list(range(group_bits))[::-1]
+
+
+def sum_scatter(block, devices, group_size, flipped):
+    left = list(range(devices.bit_length() - 1))[::-1]
+    columns = block.shape[1]
+    for bit in bit_order(devices, group_size, flipped):
+        before = 2 ** left.index(bit)
+        view = block.reshape(before, 2, -1, columns)
+        own = own_bit(bit, group_size)
+        kept = lax.dynamic_index_in_dim(view, own, 1, keepdims=False)
+        sent = lax.dynamic_index_in_dim(view, 1 - own, 1, keepdims=False)
+        left.remove(bit)
+        arrived = exchange(sent, bit, devices)
+        block = kept.astype(jnp.float32) + arrived.astype(jnp.float32)
+        if left:
+            block = block.astype(jnp.bfloat16)
+        block = block.reshape(-1, columns)
+    return block
+
+
+def gather_rows(block, devices, group_size, flipped):
+    held = []
+    columns = block.shape[1]
+    for bit in bit_order(devices, group_size, flipped)[::-1]:
+        arrived = exchange(block, bit, devices)
+        held = sorted(held + [bit], reverse=True)
+        before = 2 ** held.index(bit)
+        first = own_bit(bit, group_size) == 0
+        low = jnp.where(first, block, arrived).reshape(before, -1, columns)
+        high = jnp.where(first, arrived, block).reshape(before, -1, columns)
+        block = jnp.stack([low, high], axis=1).reshape(-1, columns)
+    return block
 
 
 def adam_step(weight, gradient, moment_one, moment_two, decay_rate, step_rate):
@@ -198,6 +262,8 @@
 
 
 def per_device(
+    devices,
+    group_size,
     tokens,
     cotangent,
     seq_lens,
@@ -217,18 +283,24 @@
     second_down,
     second_vec,
 ):
-    axes = ("dp", "group")
-    shards = D // (w_out.shape[0] // D)
-
-    def gather(shard, rows):
-        low = shard.astype(jnp.bfloat16).reshape(rows // shards, -1)
-        return lax.all_gather(low, axes, axis=0, tiled=True)
-
-    weight_qkv = gather(w_qkv, D)
-    weight_out = gather(w_out, D)
-    weight_up = gather(w_up, D)
-    weight_down = gather(w_down, FF)
-    packed = lax.all_gather(vectors.astype(jnp.bfloat16), axes, axis=0, tiled=True).astype(jnp.float32)
+    shard_rows = w_out.shape[0] // D
+    low_qkv = w_qkv.astype(jnp.bfloat16).reshape(shard_rows, 3 * D)
+    low_out = w_out.astype(jnp.bfloat16).reshape(shard_rows, D)
+    low_up = w_up.astype(jnp.bfloat16).reshape(shard_rows, FF)
+    low_down = w_down.astype(jnp.bfloat16).reshape(-1, D)
+    low_vec = vectors.astype(jnp.bfloat16).reshape(shard_rows, -1)
+    vec_width = low_vec.shape[1]
+    vec_pad = ((0, 0), (0, 128 - vec_width))
+    low_up = jnp.concatenate([low_up, jnp.pad(low_vec, vec_pad)], axis=1)
+    low_late = jnp.concatenate([low_qkv[:, 2 * D :], low_out], axis=1)
+    full_up = gather_rows(low_up, devices, group_size, False)
+    weight_down = gather_rows(low_down, devices, group_size, True)
+    full_early = gather_rows(low_qkv[:, : 2 * D], devices, group_size, False)
+    full_late = gather_rows(low_late, devices, group_size, True)
+    weight_up = full_up[:, :FF]
+    packed = full_up[:, FF : FF + vec_width].reshape(-1).astype(jnp.float32)
+    weight_qkv = jnp.concatenate([full_early, full_late[:, :D]], axis=1)
+    weight_out = full_late[:, D:]
     gain_one = packed[0:D]
     gain_two = packed[D : 2 * D]
     shift_one = packed[2 * D : 3 * D]
@@ -293,17 +365,25 @@
             seed_total,
         ]
     )
-    def scatter(gradient):
-        low = gradient.astype(jnp.bfloat16)
-        part = lax.psum_scatter(low, axes, scatter_dimension=0, tiled=True)
-        return part.astype(jnp.float32).reshape(-1)
-
+    grad_early = grad_qkv[:, : 2 * D].astype(jnp.bfloat16)
+    grad_late = jnp.concatenate(
+        [
+            grad_qkv[:, 2 * D :].astype(jnp.bfloat16),
+            grad_out.astype(jnp.bfloat16),
+            jnp.pad(grad_vec.reshape(D, -1), vec_pad).astype(jnp.bfloat16),
+        ],
+        axis=1,
+    )
+    sum_up = sum_scatter(grad_up.astype(jnp.bfloat16), devices, group_size, False)
+    sum_down = sum_scatter(grad_down.astype(jnp.bfloat16), devices, group_size, True)
+    sum_early = sum_scatter(grad_early, devices, group_size, False)
+    sum_late = sum_scatter(grad_late, devices, group_size, True)
     summed = (
-        scatter(grad_qkv),
-        scatter(grad_out),
-        scatter(grad_up),
-        scatter(grad_down),
-        lax.psum_scatter(grad_vec, axes, scatter_dimension=0, tiled=True),
+        jnp.concatenate([sum_early, sum_late[:, :D]], axis=1).reshape(-1),
+        sum_late[:, D : 2 * D].reshape(-1),
+        sum_up.reshape(-1),
+        sum_down.reshape(-1),
+        sum_late[:, 2 * D : 2 * D + vec_width].reshape(-1),
     )
     masters = (w_qkv, w_out, w_up, w_down, vectors)
     firsts = (first_qkv, first_out, first_up, first_down, first_vec)
@@ -358,8 +438,10 @@
         P(("dp", "group")),
         P(("dp", "group")),
     )
+    group_size = mesh.shape["group"]
+    devices = mesh.shape["dp"] * group_size
     return jax.shard_map(
-        per_device,
+        functools.partial(per_device, devices, group_size),
         mesh=mesh,
         in_specs=placed,
         out_specs=(

time: 736 us -> 539 us (0.73)
  waiting for transfers between devices: 373 us -> 214 us
  blocking collectives: 82.9 us -> 0 us
  starting transfers between devices: 0.33 us -> 39.8 us
  other arithmetic: 31.7 us -> 63.4 us
  between operations: 14.8 us -> 2.53 us
  matrix products: 113 us -> 104 us
    reduce_scatter x4 -> x0, waiting for transfers between devices: 250 us -> none  [scatter(): part = lax.psum_scatter(low, axes, scatter_dimension=0, tiled=True)]
    ppermute x0 -> x40, waiting for transfers between devices: none -> 214 us  [exchange(): return lax.ppermute(block, ('dp', 'group'), pairs)]
    all_gather x4 -> x0, waiting for transfers between devices: 123 us -> none  [gather(): return lax.all_gather(low, axes, axis=0, tiled=True)]
    unnamed x2 -> x0, blocking collectives: 82.9 us -> none
    ppermute x0 -> x40, starting transfers between devices: none -> 39.8 us  [exchange(): return lax.ppermute(block, ('dp', 'group'), pairs)]
    another operation x1 -> x34, other arithmetic: 0.18 us -> 14.5 us  [the longest x33 14.3 us: gather_rows(): block = jnp.stack([low, high], axis=1).reshape(-1, columns)]
    concatenate x3, local copies, waits for them, and re-layouts: 19 us -> 7.68 us  [the longest x1 3 us: lane_tables(): jnp.concatenate([cosines, cosines, ones] * 2, axis=-1)]
    convert_element_type x4 -> x21, other arithmetic: 3.62 us -> 12.8 us  [the longest x16 9.15 us: sum_scatter(): block = block.astype(jnp.bfloat16)]
  transfers between devices with their start and end apart: 8 -> 40, of which waited for: 7 -> 23; matrix products, arithmetic and copies ran while one was open for 20% -> 26% of each run, Pallas kernels for 11% -> 14%
where the time goes in v2:
time: 539 us; the launch traced here: 533 us
  waiting for transfers between devices  214 us (40%)
  matrix products  104 us (19%)
  Pallas kernels  76.2 us (14%)
  other arithmetic  63.4 us (12%)
  starting transfers between devices  39.8 us (7%)
  local copies, waits for them, and re-layouts  32.9 us (6%)
    ppermute x40, waiting for transfers between devices, exchange(): return lax.ppermute(block, ('dp', 'group'), pairs)  214 us
    pallas_call x1, Pallas kernels, attention(): pl.pallas_call(attention_kernel, grid=(pairs,), in_specs=[whole(1, TOK_DE...  76.2 us
    ppermute x40, starting transfers between devices, exchange(): return lax.ppermute(block, ('dp', 'group'), pairs)  39.8 us
    dot_general x1, matrix products, per_device(): jnp.dot(normed_two, weight_up, preferred_element_type=jnp.float32) + bias_up  36.1 us
    dot_general x1, matrix products, per_device(): jnp.einsum('td,fd->tf', seed_rows, weight_down, preferred_element_type=jn...  16.8 us
    another operation x33, other arithmetic, gather_rows(): block = jnp.stack([low, high], axis=1).reshape(-1, columns)  14.3 us
  transfers between devices with their start and end apart: 40, of which 23 were waited for; matrix products, arithmetic and copies ran while one was open for 26% of the time, Pallas kernels for 14%

profile of v2, /device:TPU:0, one launch (start us, length us, event | category | flops | bytes accessed | tf_op | source)
XLA Modules:
  0.0 533.4 jit_solution(4468033669068113494)
XLA Ops:
  18.9 9.9 %collective-permute-done.1 = bf16[48,3200]{1,0:T(8,128)(2,1)} collective-permute-done((bf16[48,3200]{1,0:T(8,128)(2,1)S(1)}, bf16[48,3200]{1,0:T(8,128)(2,1)}, u32[]{:S(2)}, u32[]{:S(2)}) %collective-permute-start.1) | collective-permute-done | bytes 307232 | tf_op jit(solution)/shard_map/ppermute | solution.py:204
  32.6 12.5 %collective-permute-done.2 = bf16[96,3200]{1,0:T(8,128)(2,1)S(1)} collective-permute-done((bf16[96,3200]{1,0:T(8,128)(2,1)S(1)}, bf16[96,3200]{1,0:T(8,128)(2,1)S(1)}, u32[]{:S(2)}, u32[]{:S(2)}) %collective-permute-start.2) | collective-permute-done | bytes 614432 | tf_op jit(solution)/shard_map/ppermute | solution.py:204
  48.0 7.0 %collective-permute-done.6 = bf16[48,1536]{1,0:T(8,128)(2,1)S(1)} collective-permute-done((bf16[48,1536]{1,0:T(8,128)(2,1)S(1)}, bf16[48,1536]{1,0:T(8,128)(2,1)S(1)}, u32[]{:S(2)}, u32[]{:S(2)}) %collective-permute-start.6) | collective-permute-done | bytes 147488 | tf_op jit(solution)/shard_map/ppermute | solution.py:204
  55.1 17.7 %collective-permute-done.3 = bf16[192,3200]{1,0:T(8,128)(2,1)S(1)} collective-permute-done((bf16[192,3200]{1,0:T(8,128)(2,1)S(1)}, bf16[192,3200]{1,0:T(8,128)(2,1)S(1)}, u32[]{:S(2)}, u32[]{:S(2)}) %collective-permute-start.3) | collective-permute-done | bytes 1228832 | tf_op jit(solution)/shard_map/ppermute | solution.py:204
  77.2 5.7 %collective-permute-done.7 = bf16[96,1536]{1,0:T(8,128)(2,1)S(1)} collective-permute-done((bf16[96,1536]{1,0:T(8,128)(2,1)S(1)}, bf16[96,1536]{1,0:T(8,128)(2,1)S(1)}, u32[]{:S(2)}, u32[]{:S(2)}) %collective-permute-start.7) | collective-permute-done | bytes 294944 | tf_op jit(solution)/shard_map/ppermute | solution.py:204
  87.1 10.9 %collective-permute-done.8 = bf16[192,1536]{1,0:T(8,128)(2,1)S(1)} collective-permute-done((bf16[192,1536]{1,0:T(8,128)(2,1)S(1)}, bf16[192,1536]{1,0:T(8,128)(2,1)S(1)}, u32[]{:S(2)}, u32[]{:S(2)}) %collective-permute-start.8) | collective-permute-done | bytes 589856 | tf_op jit(solution)/shard_map/ppermute | solution.py:204
  105.5 36.1 %multiply_convert_fusion = (bf16[1024,3072]{1,0:T(8,128)(2,1)S(1)}, f32[1024,3072]{1,0:T(8,128)}, f32[1024,3072]{1,0:T(8,128)}) fusion(f32[3072]{0:T(1024)S(1)} %slice.95, bf16[768,3200]{1,0:T(8,128)(2,1)} %bitcast.271, bf16[1024,768]{1,0:T(8,128)(2,1)S(1)} %copy-done, f32[768]{0:T(1024)S(1)} %get-tuple-element.99, f32[768]{0:T(1024)S(1)} %get-tuple-element.100, ...), kind=kOutput, calls=%fused_computation.3 | convolution fusion | flops 5044174848 | bytes 37775360 | tf_op jit(solution)/shard_map/dot_general | solution.py:330
  141.6 5.6 %convolution_convert_fusion = bf16[3072,768]{1,0:T(8,128)(2,1)S(1)} fusion(bf16[1024,3072]{1,0:T(8,128)(2,1)S(1)} %get-tuple-element.50, bf16[1024,768]{1,0:T(8,128)(2,1)S(1)} %get-tuple-element.49.seed_ref), kind=kOutput, calls=%fused_computation.19 | convolution fusion | flops 4834197504 | bytes 12582912 | tf_op jit(solution)/shard_map/tf,td->fd/dot_general | solution.py:340
  150.5 3.2 multiply_sine_fusion
  173.4 24.3 %collective-permute-done.36 = bf16[1,768,768]{2,1,0:T(8,128)(2,1)S(1)} collective-permute-done((bf16[1,768,768]{2,1,0:T(8,128)(2,1)S(1)}, bf16[1,768,768]{2,1,0:T(8,128)(2,1)S(1)}, u32[]{:S(2)}, u32[]{:S(2)}) %collective-permute-start.36) | collective-permute-done | bytes 1179680 | tf_op jit(solution)/shard_map/ppermute | solution.py:204
  203.5 8.8 %collective-permute-done.37 = bf16[1,384,768]{2,1,0:T(8,128)(2,1)S(1)} collective-permute-done((bf16[1,384,768]{2,1,0:T(8,128)(2,1)S(1)}, bf16[1,384,768]{2,1,0:T(8,128)(2,1)S(1)}, u32[]{:S(2)}, u32[]{:S(2)}) %collective-permute-start.37) | collective-permute-done | bytes 589856 | tf_op jit(solution)/shard_map/ppermute | solution.py:204
  212.6 76.2 %shard_map.305 = (bf16[1024,768]{1,0:T(8,128)(2,1)}, bf16[1024,2304]{1,0:T(8,128)(2,1)}) custom-call(s32[1,1024]{1,0:T(1,128)S(1)} %subtract_subtract_fusion.begins_ref, bf16[1024,768]{1,0:T(8,128)(2,1)} %fusion.24.normed_ref, bf16[1024,768]{1,0:T(8,128)(2,1)} %copy-done.8, bf16[768,2304]{1,0:T(8,128)(2,1)} %pad_maximum_fusion.2.weight_ref, ...), custom_call_target="tpu_custom_call" | custom-call | flops 16000000000 | bytes 20000000 | tf_op jit(solution)/shard_map/pallas_call | solution.py:172
  291.3 6.6 %convolution_convert_fusion.2 = bf16[768,2304]{1,0:T(8,128)(2,1)S(1)} fusion(bf16[1024,768]{1,0:T(8,128)(2,1)S(1)} %copy-done.21, bf16[1024,2304]{1,0:T(8,128)(2,1)} %get-tuple-element.20), kind=kOutput, calls=%fused_computation.21 | convolution fusion | flops 3625648128 | bytes 9830400 | tf_op jit(solution)/shard_map/td,te->de/dot_general | solution.py:346
  304.3 3.5 collective-permute-done.15
  308.5 12.5 %collective-permute-done.16 = bf16[192,768]{1,0:T(8,128)(2,1)S(1)} collective-permute-done((bf16[192,768]{1,0:T(8,128)(2,1)S(1)}, bf16[192,768]{1,0:T(8,128)(2,1)S(1)}, u32[]{:S(2)}, u32[]{:S(2)}) %collective-permute-start.16) | collective-permute-done | bytes 294944 | tf_op jit(solution)/shard_map/ppermute | solution.py:204
  323.7 13.8 %collective-permute-done.17 = bf16[384,768]{1,0:T(8,128)(2,1)S(1)} collective-permute-done((bf16[384,768]{1,0:T(8,128)(2,1)S(1)}, bf16[384,768]{1,0:T(8,128)(2,1)S(1)}, u32[]{:S(2)}, u32[]{:S(2)}) %collective-permute-start.17) | collective-permute-done | bytes 589856 | tf_op jit(solution)/shard_map/ppermute | solution.py:204
  339.3 8.6 %collective-permute-done.21 = bf16[2,96,1536]{2,1,0:T(8,128)(2,1)} collective-permute-done((bf16[2,96,1536]{2,1,0:T(8,128)(2,1)S(1)}, bf16[2,96,1536]{2,1,0:T(8,128)(2,1)}, u32[]{:S(2)}, u32[]{:S(2)}) %collective-permute-start.21) | collective-permute-done | bytes 589856 | tf_op jit(solution)/shard_map/ppermute | solution.py:204
  350.9 13.5 %collective-permute-done.18 = bf16[768,768]{1,0:T(8,128)(2,1)} collective-permute-done((bf16[768,768]{1,0:T(8,128)(2,1)S(1)}, bf16[768,768]{1,0:T(8,128)(2,1)}, u32[]{:S(2)}, u32[]{:S(2)}) %collective-permute-start.18) | collective-permute-done | bytes 1179680 | tf_op jit(solution)/shard_map/ppermute | solution.py:204
  371.0 6.3 %collective-permute-done.23 = bf16[1,48,1536]{2,1,0:T(8,128)(2,1)S(1)} collective-permute-done((bf16[1,48,1536]{2,1,0:T(8,128)(2,1)S(1)}, bf16[1,48,1536]{2,1,0:T(8,128)(2,1)S(1)}, u32[]{:S(2)}, u32[]{:S(2)}) %collective-permute-start.23) | collective-permute-done | bytes 147488 | tf_op jit(solution)/shard_map/ppermute | solution.py:204
  392.1 16.8 %fusion.80 = (bf16[3072]{0:T(1024)(128)(2,1)S(1)}, bf16[1024,3072]{1,0:T(8,128)(2,1)}) fusion(f32[1024,3072]{1,0:T(8,128)} %get-tuple-element.51, bf16[1024,768]{1,0:T(8,128)(2,1)S(1)} %copy-done.9, bf16[3072,768]{1,0:T(8,128)(2,1)} %bitcast.286, f32[1024,3072]{1,0:T(8,128)} %get-tuple-element.106, f32[3072]{0:T(1024)S(1)} %copy-done.32), kind=kOutput, calls=%fused_computation.230 | convolution fusion | flops 4882166784 | bytes 37767168 | tf_op jit(solution)/shard_map/td,fd->tf/dot_general | solution.py:342
  408.8 8.9 %fusion.9 = f32[1024,768]{1,0:T(8,128)S(1)} fusion(bf16[1024,3072]{1,0:T(8,128)(2,1)} %get-tuple-element.109, bf16[768,3200]{1,0:T(8,128)(2,1)} %bitcast.272), kind=kOutput, calls=%fused_computation.31 | convolution fusion | flops 4831838208 | bytes 14155776 | tf_op jit(solution)/shard_map/tf,df->td/dot_general | solution.py:345
  417.8 10.2 %fusion.35 = (bf16[768]{0:T(1024)(128)(2,1)S(1)}, f32[1024]{0:T(1024)S(1)}, f32[1024]{0:T(1024)S(1)}, bf16[768]{0:T(1024)(128)(2,1)S(1)}, bf16[768]{0:T(1024)(12...) fusion(bf16[1024,768]{1,0:T(8,128)(2,1)S(1)} %copy-done, ...), kind=kOutput, calls=%fused_computation.58 | convolution fusion | flops 3644318720 | bytes 16158720 | tf_op jit(solution)/shard_map/te,de->td/dot_general | solution.py:349
  433.2 6.3 %convolution_convert_fusion.1 = bf16[768,3072]{1,0:T(8,128)(2,1)S(1)} fusion(bf16[1024,3072]{1,0:T(8,128)(2,1)S(1)} %copy-done.46, bf16[1024,768]{1,0:T(8,128)(2,1)S(1)} %copy-done, f32[768]{0:T(1024)S(1)} %copy-done.37, f32[768]{0:T(1024)S(1)} %get-tuple-element.100, f32[1024]{0:T(1024)S(1)} %add_rsqrt_fusion, f32[1024]{0:T(1024)S(1)} %broadcast_multiply_fusion.4), kind=kOutput, calls=%fused_computation.20 | convolution fusion | flops 4838916096 | bytes 12597248 | tf_op jit(solution)/shard_map/td,tf->df/dot_general | solution.py:344
  441.9 8.4 %fusion.40 = bf16[1024,768]{1,0:T(8,128)(2,1)} fusion(bf16[1024,768]{1,0:T(8,128)(2,1)S(1)} %copy-done, f32[1024,768]{1,0:T(8,128)S(1)} %copy-done.44, bf16[1024,3072]{1,0:T(8,128)(2,1)} %copy-done.47, bf16[3072,768]{1,0:T(8,128)(2,1)S(1)} %bitcast.289, f32[768]{0:T(1024)S(1)} %copy-done.35, f32[768]{0:T(1024)S(1)} %copy-done.34), kind=kOutput, calls=%fused_computation.63 | convolution fusion | flops 4836556800 | bytes 17307648 | tf_op jit(solution)/shard_map/dot_general | solution.py:336
  450.3 6.7 %collective-permute-done.26 = bf16[1,192,1664]{2,1,0:T(8,128)(2,1)S(1)} collective-permute-done((bf16[1,192,1664]{2,1,0:T(8,128)(2,1)S(1)}, bf16[1,192,1664]{2,1,0:T(8,128)(2,1)S(1)}, u32[]{:S(2)}, u32[]{:S(2)}) %collective-permute-start.26) | collective-permute-done | bytes 639008 | tf_op jit(solution)/shard_map/ppermute | solution.py:204
  458.9 7.5 %collective-permute-done.27 = bf16[1,96,1664]{2,1,0:T(8,128)(2,1)S(1)} collective-permute-done((bf16[1,96,1664]{2,1,0:T(8,128)(2,1)S(1)}, bf16[1,96,1664]{2,1,0:T(8,128)(2,1)S(1)}, u32[]{:S(2)}, u32[]{:S(2)}) %collective-permute-start.27) | collective-permute-done | bytes 319520 | tf_op jit(solution)/shard_map/ppermute | solution.py:204
  472.6 3.2 collective-permute-done.28
  476.0 3.3 fusion.31
  480.5 17.4 %collective-permute-done.31 = bf16[2,96,3072]{2,1,0:T(8,128)(2,1)} collective-permute-done((bf16[2,96,3072]{2,1,0:T(8,128)(2,1)}, bf16[2,96,3072]{2,1,0:T(8,128)(2,1)}, u32[]{:S(2)}, u32[]{:S(2)}) %collective-permute-start.31) | collective-permute-done | bytes 1179680 | tf_op jit(solution)/shard_map/ppermute | solution.py:204
  504.2 8.7 %collective-permute-done.32 = bf16[1,96,3072]{2,1,0:T(8,128)(2,1)S(1)} collective-permute-done((bf16[1,96,3072]{2,1,0:T(8,128)(2,1)S(1)}, bf16[1,96,3072]{2,1,0:T(8,128)(2,1)S(1)}, u32[]{:S(2)}, u32[]{:S(2)}) %collective-permute-start.32) | collective-permute-done | bytes 589856 | tf_op jit(solution)/shard_map/ppermute | solution.py:204
  515.4 10.0 %collective-permute-done.33 = bf16[1,48,3072]{2,1,0:T(8,128)(2,1)S(1)} collective-permute-done((bf16[1,48,3072]{2,1,0:T(8,128)(2,1)S(1)}, bf16[1,48,3072]{2,1,0:T(8,128)(2,1)S(1)}, u32[]{:S(2)}, u32[]{:S(2)}) %collective-permute-start.33) | collective-permute-done | bytes 294944 | tf_op jit(solution)/shard_map/ppermute | solution.py:204
  526.2 4.5 collective-permute-done.34
  (318 shorter events, 136.4 us)
Async XLA Ops:
  2.7 10.3 %collective-permute-start = (bf16[24,3200]{1,0:T(8,128)(2,1)S(1)}, bf16[24,3200]{1,0:T(8,128)(2,1)S(1)}, u32[]{:S(2)}, u32[]{:S(2)}) collective-permute-start(bf16[24,3200]{1,0:T(8,128)(2,1)S(1)} %fusion.61), channel_id=1, source_target_pairs={{0,1},{1,0},{2,3},{3,2},{4,5},{5,4},{6,7},{7,6},{8,9},{9,8},{10,11... | collective-permute-start | bytes 460808 | tf_op jit(solution)/shard_map/ppermute | solution.py:204
  8.5 23.0 %collective-permute-start.10 = (bf16[24,1536]{1,0:T(8,128)(2,1)}, bf16[24,1536]{1,0:T(8,128)(2,1)}, u32[]{:S(2)}, u32[]{:S(2)}) collective-permute-start(bf16[24,1536]{1,0:T(8,128)(2,1)} %pad_maximum_fusion.22), channel_id=1, source_target_pairs={{0,1},{1,0},{2,3},{3,2},{4,5},{5,4},{6,7},{7,6},{8,9},{9,8},{10,11... | collective-permute-start | bytes 221192 | tf_op jit(solution)/shard_map/ppermute | solution.py:204
  9.2 37.8 %collective-permute-start.5 = (bf16[24,1536]{1,0:T(8,128)(2,1)}, bf16[24,1536]{1,0:T(8,128)(2,1)}, u32[]{:S(2)}, u32[]{:S(2)}) collective-permute-start(bf16[24,1536]{1,0:T(8,128)(2,1)} %slice.86), channel_id=1, source_target_pairs={{0,1},{1,0},{2,3},{3,2},{4,5},{5,4},{6,7},{7,6},{8,9},{9,8},{10,11... | collective-permute-start | bytes 221192 | tf_op jit(solution)/shard_map/ppermute | solution.py:204
  13.1 15.7 %collective-permute-start.1 = (bf16[48,3200]{1,0:T(8,128)(2,1)S(1)}, bf16[48,3200]{1,0:T(8,128)(2,1)}, u32[]{:S(2)}, u32[]{:S(2)}) collective-permute-start(bf16[48,3200]{1,0:T(8,128)(2,1)S(1)} %bitcast.311), channel_id=1, source_target_pairs={{0,2},{1,3},{2,0},{3,1},{4,6},{5,7},{6,4},{7,5},{8,10},{9,11},{10,... | collective-permute-start | bytes 921608 | tf_op jit(solution)/shard_map/ppermute | solution.py:204
  29.9 15.1 %collective-permute-start.2 = (bf16[96,3200]{1,0:T(8,128)(2,1)S(1)}, bf16[96,3200]{1,0:T(8,128)(2,1)S(1)}, u32[]{:S(2)}, u32[]{:S(2)}) collective-permute-start(bf16[96,3200]{1,0:T(8,128)(2,1)S(1)} %bitcast.300), channel_id=1, source_target_pairs={{0,16},{1,17},{2,18},{3,19},{4,20},{5,21},{6,22},{7,23},{8,24},{9,... | collective-permute-start | bytes 1843208 | tf_op jit(solution)/shard_map/ppermute | solution.py:204
  32.5 15.5 %collective-permute-start.11 = (bf16[48,1536]{1,0:T(8,128)(2,1)S(1)}, bf16[48,1536]{1,0:T(8,128)(2,1)S(1)}, u32[]{:S(2)}, u32[]{:S(2)}) collective-permute-start(bf16[48,1536]{1,0:T(8,128)(2,1)S(1)} %bitcast.324), channel_id=1, source_target_pairs={{0,2},{1,3},{2,0},{3,1},{4,6},{5,7},{6,4},{7,5},{8,10},{9,11},{10,... | collective-permute-start | bytes 442376 | tf_op jit(solution)/shard_map/ppermute | solution.py:204
  45.4 27.4 %collective-permute-start.3 = (bf16[192,3200]{1,0:T(8,128)(2,1)S(1)}, bf16[192,3200]{1,0:T(8,128)(2,1)S(1)}, u32[]{:S(2)}, u32[]{:S(2)}) collective-permute-start(bf16[192,3200]{1,0:T(8,128)(2,1)S(1)} %bitcast.275), channel_id=1, source_target_pairs={{0,8},{1,9},{2,10},{3,11},{4,12},{5,13},{6,14},{7,15},{8,0},{9,1},... | collective-permute-start | bytes 3686408 | tf_op jit(solution)/shard_map/ppermute | solution.py:204
  73.3 25.9 %collective-permute-start.4 = (bf16[384,3200]{1,0:T(8,128)(2,1)S(1)}, bf16[384,3200]{1,0:T(8,128)(2,1)S(1)}, u32[]{:S(2)}, u32[]{:S(2)}) collective-permute-start(bf16[384,3200]{1,0:T(8,128)(2,1)S(1)} %bitcast.255), channel_id=1, source_target_pairs={{0,4},{1,5},{2,6},{3,7},{4,0},{5,1},{6,2},{7,3},{8,12},{9,13},{10,... | collective-permute-start | bytes 7372808 | tf_op jit(solution)/shard_map/ppermute | solution.py:204
  73.4 9.5 %collective-permute-start.7 = (bf16[96,1536]{1,0:T(8,128)(2,1)S(1)}, bf16[96,1536]{1,0:T(8,128)(2,1)S(1)}, u32[]{:S(2)}, u32[]{:S(2)}) collective-permute-start(bf16[96,1536]{1,0:T(8,128)(2,1)S(1)} %bitcast.319), channel_id=1, source_target_pairs={{0,16},{1,17},{2,18},{3,19},{4,20},{5,21},{6,22},{7,23},{8,24},{9,... | collective-permute-start | bytes 884744 | tf_op jit(solution)/shard_map/ppermute | solution.py:204
  75.7 9.2 %collective-permute-start.12 = (bf16[96,1536]{1,0:T(8,128)(2,1)S(1)}, bf16[96,1536]{1,0:T(8,128)(2,1)S(1)}, u32[]{:S(2)}, u32[]{:S(2)}) collective-permute-start(bf16[96,1536]{1,0:T(8,128)(2,1)S(1)} %bitcast.318), channel_id=1, source_target_pairs={{0,8},{1,9},{2,10},{3,11},{4,12},{5,13},{6,14},{7,15},{8,0},{9,1},... | collective-permute-start | bytes 884744 | tf_op jit(solution)/shard_map/ppermute | solution.py:204
  83.0 15.0 %collective-permute-start.8 = (bf16[192,1536]{1,0:T(8,128)(2,1)S(1)}, bf16[192,1536]{1,0:T(8,128)(2,1)S(1)}, u32[]{:S(2)}, u32[]{:S(2)}) collective-permute-start(bf16[192,1536]{1,0:T(8,128)(2,1)S(1)} %bitcast.301), channel_id=1, source_target_pairs={{0,8},{1,9},{2,10},{3,11},{4,12},{5,13},{6,14},{7,15},{8,0},{9,1},... | collective-permute-start | bytes 1769480 | tf_op jit(solution)/shard_map/ppermute | solution.py:204
  85.8 76.6 %collective-permute-start.13 = (bf16[192,1536]{1,0:T(8,128)(2,1)}, bf16[192,1536]{1,0:T(8,128)(2,1)}, u32[]{:S(2)}, u32[]{:S(2)}) collective-permute-start(bf16[192,1536]{1,0:T(8,128)(2,1)} %bitcast.42), channel_id=1, source_target_pairs={{0,16},{1,17},{2,18},{3,19},{4,20},{5,21},{6,22},{7,23},{8,24},{9,... | collective-permute-start | bytes 1769480 | tf_op jit(solution)/shard_map/ppermute | solution.py:204
  148.8 18.0 %collective-permute-start.35 = (bf16[4,384,768]{2,1,0:T(8,128)(2,1)}, bf16[4,384,768]{2,1,0:T(8,128)(2,1)}, u32[]{:S(2)}, u32[]{:S(2)}) collective-permute-start(bf16[4,384,768]{2,1,0:T(8,128)(2,1)} %dynamic-slice_bitcast_fusion), channel_id=1, source_target_pairs={{0,4},{1,5},{2,6},{3,7},{4,0},{5,1},{6,2},{7,3},{8,12},{9,13},{10,... | collective-permute-start | bytes 7077896 | tf_op jit(solution)/shard_map/ppermute | solution.py:204
  150.5 14.0 %collective-permute-start.9 = (bf16[384,1536]{1,0:T(8,128)(2,1)}, bf16[384,1536]{1,0:T(8,128)(2,1)}, u32[]{:S(2)}, u32[]{:S(2)}) collective-permute-start(bf16[384,1536]{1,0:T(8,128)(2,1)} %bitcast.30), channel_id=1, source_target_pairs={{0,4},{1,5},{2,6},{3,7},{4,0},{5,1},{6,2},{7,3},{8,12},{9,13},{10,... | collective-permute-start | bytes 3538952 | tf_op jit(solution)/shard_map/ppermute | solution.py:204
  170.0 27.7 %collective-permute-start.36 = (bf16[1,768,768]{2,1,0:T(8,128)(2,1)S(1)}, bf16[1,768,768]{2,1,0:T(8,128)(2,1)S(1)}, u32[]{:S(2)}, u32[]{:S(2)}) collective-permute-start(bf16[1,768,768]{2,1,0:T(8,128)(2,1)S(1)} %dynamic-slice_bitcast_fusion.3), channel_id=1, source_target_pairs={{0,16},{1,17},{2,18},{3,19},{4,20},{5,21},{6,22},{7,23},{8,24},{9,... | collective-permute-start | bytes 3538952 | tf_op jit(solution)/shard_map/ppermute | solution.py:204
  198.1 14.2 %collective-permute-start.37 = (bf16[1,384,768]{2,1,0:T(8,128)(2,1)S(1)}, bf16[1,384,768]{2,1,0:T(8,128)(2,1)S(1)}, u32[]{:S(2)}, u32[]{:S(2)}) collective-permute-start(bf16[1,384,768]{2,1,0:T(8,128)(2,1)S(1)} %dynamic-slice_bitcast_fusion.7), channel_id=1, source_target_pairs={{0,8},{1,9},{2,10},{3,11},{4,12},{5,13},{6,14},{7,15},{8,0},{9,1},... | collective-permute-start | bytes 1769480 | tf_op jit(solution)/shard_map/ppermute | solution.py:204
  212.5 76.3 %collective-permute-start.38 = (bf16[1,192,768]{2,1,0:T(8,128)(2,1)S(1)}, bf16[1,192,768]{2,1,0:T(8,128)(2,1)S(1)}, u32[]{:S(2)}, u32[]{:S(2)}) collective-permute-start(bf16[1,192,768]{2,1,0:T(8,128)(2,1)S(1)} %dynamic-slice_bitcast_fusion.10), channel_id=1, source_target_pairs={{0,2},{1,3},{2,0},{3,1},{4,6},{5,7},{6,4},{7,5},{8,10},{9,11},{10,... | collective-permute-start | bytes 884744 | tf_op jit(solution)/shard_map/ppermute | solution.py:204
  288.8 12.4 %collective-permute-start.39 = (bf16[1,96,768]{2,1,0:T(8,128)(2,1)S(1)}, bf16[1,96,768]{2,1,0:T(8,128)(2,1)S(1)}, u32[]{:S(2)}, u32[]{:S(2)}) collective-permute-start(bf16[1,96,768]{2,1,0:T(8,128)(2,1)S(1)} %dynamic-slice_bitcast_fusion.13), channel_id=1, source_target_pairs={{0,1},{1,0},{2,3},{3,2},{4,5},{5,4},{6,7},{7,6},{8,9},{9,8},{10,11... | collective-permute-start | bytes 442376 | tf_op jit(solution)/shard_map/ppermute | solution.py:204
  304.2 18.5 %collective-permute-start.20 = (bf16[4,96,1536]{2,1,0:T(8,128)(2,1)S(1)}, bf16[4,96,1536]{2,1,0:T(8,128)(2,1)S(1)}, u32[]{:S(2)}, u32[]{:S(2)}) collective-permute-start(bf16[4,96,1536]{2,1,0:T(8,128)(2,1)S(1)} %dynamic-slice_bitcast_fusion.5), channel_id=1, source_target_pairs={{0,4},{1,5},{2,6},{3,7},{4,0},{5,1},{6,2},{7,3},{8,12},{9,13},{10,... | collective-permute-start | bytes 3538952 | tf_op jit(solution)/shard_map/ppermute | solution.py:204
  307.9 13.2 %collective-permute-start.16 = (bf16[192,768]{1,0:T(8,128)(2,1)S(1)}, bf16[192,768]{1,0:T(8,128)(2,1)S(1)}, u32[]{:S(2)}, u32[]{:S(2)}) collective-permute-start(bf16[192,768]{1,0:T(8,128)(2,1)S(1)} %bitcast.320), channel_id=1, source_target_pairs={{0,2},{1,3},{2,0},{3,1},{4,6},{5,7},{6,4},{7,5},{8,10},{9,11},{10,... | collective-permute-start | bytes 884744 | tf_op jit(solution)/shard_map/ppermute | solution.py:204
  321.2 16.3 %collective-permute-start.17 = (bf16[384,768]{1,0:T(8,128)(2,1)S(1)}, bf16[384,768]{1,0:T(8,128)(2,1)S(1)}, u32[]{:S(2)}, u32[]{:S(2)}) collective-permute-start(bf16[384,768]{1,0:T(8,128)(2,1)S(1)} %bitcast.302), channel_id=1, source_target_pairs={{0,8},{1,9},{2,10},{3,11},{4,12},{5,13},{6,14},{7,15},{8,0},{9,1},... | collective-permute-start | bytes 1769480 | tf_op jit(solution)/shard_map/ppermute | solution.py:204
  323.1 24.8 %collective-permute-start.21 = (bf16[2,96,1536]{2,1,0:T(8,128)(2,1)S(1)}, bf16[2,96,1536]{2,1,0:T(8,128)(2,1)}, u32[]{:S(2)}, u32[]{:S(2)}) collective-permute-start(bf16[2,96,1536]{2,1,0:T(8,128)(2,1)S(1)} %dynamic-slice_bitcast_fusion.8), channel_id=1, source_target_pairs={{0,8},{1,9},{2,10},{3,11},{4,12},{5,13},{6,14},{7,15},{8,0},{9,1},... | collective-permute-start | bytes 1769480 | tf_op jit(solution)/shard_map/ppermute | solution.py:204
  337.7 26.6 %collective-permute-start.18 = (bf16[768,768]{1,0:T(8,128)(2,1)S(1)}, bf16[768,768]{1,0:T(8,128)(2,1)}, u32[]{:S(2)}, u32[]{:S(2)}) collective-permute-start(bf16[768,768]{1,0:T(8,128)(2,1)S(1)} %bitcast.285), channel_id=1, source_target_pairs={{0,16},{1,17},{2,18},{3,19},{4,20},{5,21},{6,22},{7,23},{8,24},{9,... | collective-permute-start | bytes 3538952 | tf_op jit(solution)/shard_map/ppermute | solution.py:204
  349.3 18.1 %collective-permute-start.22 = (bf16[1,96,1536]{2,1,0:T(8,128)(2,1)S(1)}, bf16[1,96,1536]{2,1,0:T(8,128)(2,1)S(1)}, u32[]{:S(2)}, u32[]{:S(2)}) collective-permute-start(bf16[1,96,1536]{2,1,0:T(8,128)(2,1)S(1)} %constant_dynamic-slice_fusion.1), channel_id=1, source_target_pairs={{0,16},{1,17},{2,18},{3,19},{4,20},{5,21},{6,22},{7,23},{8,24},{9,... | collective-permute-start | bytes 884744 | tf_op jit(solution)/shard_map/ppermute | solution.py:204
  367.4 19.4 %collective-permute-start.19 = (bf16[1536,768]{1,0:T(8,128)(2,1)}, bf16[1536,768]{1,0:T(8,128)(2,1)}, u32[]{:S(2)}, u32[]{:S(2)}) collective-permute-start(bf16[1536,768]{1,0:T(8,128)(2,1)} %bitcast.60), channel_id=1, source_target_pairs={{0,4},{1,5},{2,6},{3,7},{4,0},{5,1},{6,2},{7,3},{8,12},{9,13},{10,... | collective-permute-start | bytes 7077896 | tf_op jit(solution)/shard_map/ppermute | solution.py:204
  367.5 9.7 %collective-permute-start.23 = (bf16[1,48,1536]{2,1,0:T(8,128)(2,1)S(1)}, bf16[1,48,1536]{2,1,0:T(8,128)(2,1)S(1)}, u32[]{:S(2)}, u32[]{:S(2)}) collective-permute-start(bf16[1,48,1536]{2,1,0:T(8,128)(2,1)S(1)} %dynamic-slice_bitcast_fusion.15), channel_id=1, source_target_pairs={{0,2},{1,3},{2,0},{3,1},{4,6},{5,7},{6,4},{7,5},{8,10},{9,11},{10,... | collective-permute-start | bytes 442376 | tf_op jit(solution)/shard_map/ppermute | solution.py:204
  439.7 29.3 %collective-permute-start.30 = (bf16[4,96,3072]{2,1,0:T(8,128)(2,1)S(1)}, bf16[4,96,3072]{2,1,0:T(8,128)(2,1)S(1)}, u32[]{:S(2)}, u32[]{:S(2)}) collective-permute-start(bf16[4,96,3072]{2,1,0:T(8,128)(2,1)S(1)} %dynamic-slice_bitcast_fusion.1), channel_id=1, source_target_pairs={{0,4},{1,5},{2,6},{3,7},{4,0},{5,1},{6,2},{7,3},{8,12},{9,13},{10,... | collective-permute-start | bytes 7077896 | tf_op jit(solution)/shard_map/ppermute | solution.py:204
  440.2 16.8 %collective-permute-start.26 = (bf16[1,192,1664]{2,1,0:T(8,128)(2,1)S(1)}, bf16[1,192,1664]{2,1,0:T(8,128)(2,1)S(1)}, u32[]{:S(2)}, u32[]{:S(2)}) collective-permute-start(bf16[1,192,1664]{2,1,0:T(8,128)(2,1)S(1)} %dynamic-slice_bitcast_fusion.6), channel_id=1, source_target_pairs={{0,16},{1,17},{2,18},{3,19},{4,20},{5,21},{6,22},{7,23},{8,24},{9,... | collective-permute-start | bytes 1916936 | tf_op jit(solution)/shard_map/ppermute | solution.py:204
  466.5 9.3 %collective-permute-start.28 = (bf16[1,48,1664]{2,1,0:T(8,128)(2,1)S(1)}, bf16[1,48,1664]{2,1,0:T(8,128)(2,1)S(1)}, u32[]{:S(2)}, u32[]{:S(2)}) collective-permute-start(bf16[1,48,1664]{2,1,0:T(8,128)(2,1)S(1)} %dynamic-slice_bitcast_fusion.12), channel_id=1, source_target_pairs={{0,2},{1,3},{2,0},{3,1},{4,6},{5,7},{6,4},{7,5},{8,10},{9,11},{10,... | collective-permute-start | bytes 479240 | tf_op jit(solution)/shard_map/ppermute | solution.py:204
  471.1 26.8 %collective-permute-start.31 = (bf16[2,96,3072]{2,1,0:T(8,128)(2,1)}, bf16[2,96,3072]{2,1,0:T(8,128)(2,1)}, u32[]{:S(2)}, u32[]{:S(2)}) collective-permute-start(bf16[2,96,3072]{2,1,0:T(8,128)(2,1)} %dynamic-slice_bitcast_fusion.4), channel_id=1, source_target_pairs={{0,8},{1,9},{2,10},{3,11},{4,12},{5,13},{6,14},{7,15},{8,0},{9,1},... | collective-permute-start | bytes 3538952 | tf_op jit(solution)/shard_map/ppermute | solution.py:204
  500.0 12.9 %collective-permute-start.32 = (bf16[1,96,3072]{2,1,0:T(8,128)(2,1)S(1)}, bf16[1,96,3072]{2,1,0:T(8,128)(2,1)S(1)}, u32[]{:S(2)}, u32[]{:S(2)}) collective-permute-start(bf16[1,96,3072]{2,1,0:T(8,128)(2,1)S(1)} %constant_dynamic-slice_fusion), channel_id=1, source_target_pairs={{0,16},{1,17},{2,18},{3,19},{4,20},{5,21},{6,22},{7,23},{8,24},{9,... | collective-permute-start | bytes 1769480 | tf_op jit(solution)/shard_map/ppermute | solution.py:204
  513.2 12.3 %collective-permute-start.33 = (bf16[1,48,3072]{2,1,0:T(8,128)(2,1)S(1)}, bf16[1,48,3072]{2,1,0:T(8,128)(2,1)S(1)}, u32[]{:S(2)}, u32[]{:S(2)}) collective-permute-start(bf16[1,48,3072]{2,1,0:T(8,128)(2,1)S(1)} %dynamic-slice_bitcast_fusion.11), channel_id=1, source_target_pairs={{0,2},{1,3},{2,0},{3,1},{4,6},{5,7},{6,4},{7,5},{8,10},{9,11},{10,... | collective-permute-start | bytes 884744 | tf_op jit(solution)/shard_map/ppermute | solution.py:204
  (61 other events, 808.0 us)

commit v3 on v2

--- a/solution.py
+++ b/solution.py
@@ -166,9 +166,8 @@
     ).astype(jnp.bfloat16)
 
 
-def attention(begins, normed, seed_rows, weight_qkv, bias_qkv, weight_out, tables):
+def attention(begins, normed, seed_rows, weight_qkv, bias_qkv, weight_out, tables, first, pairs):
     whole = lambda rows, columns: pl.BlockSpec((rows, columns), lambda j: (0, 0))
-    pairs = HEADS // 2
     return pl.pallas_call(
         attention_kernel,
         grid=(pairs,),
@@ -176,9 +175,9 @@
             whole(1, TOK_DEV),
             whole(TOK_DEV, D),
             whole(TOK_DEV, D),
-            pl.BlockSpec((D, TRIPLE), lambda j: (0, j)),
-            pl.BlockSpec((1, TRIPLE), lambda j: (0, j)),
-            pl.BlockSpec((PAIR, D), lambda j: (j, 0)),
+            pl.BlockSpec((D, TRIPLE), lambda j: (0, j + first)),
+            pl.BlockSpec((1, TRIPLE), lambda j: (0, j + first)),
+            pl.BlockSpec((PAIR, D), lambda j: (j + first, 0)),
             whole(TOK_DEV, PAIR),
             whole(TOK_DEV, PAIR),
             whole(TOK_DEV, PAIR),
@@ -188,13 +187,13 @@
             pl.BlockSpec((TOK_DEV, TRIPLE), lambda j: (0, j)),
         ],
         out_shape=[
-            jax.ShapeDtypeStruct((TOK_DEV, D), jnp.bfloat16),
-            jax.ShapeDtypeStruct((TOK_DEV, 3 * D), jnp.bfloat16),
+            jax.ShapeDtypeStruct((TOK_DEV, pairs * PAIR), jnp.bfloat16),
+            jax.ShapeDtypeStruct((TOK_DEV, pairs * TRIPLE), jnp.bfloat16),
         ],
         scratch_shapes=[pltpu.VMEM((TOK_DEV, TRIPLE), jnp.float32)] * 4,
         compiler_params=pltpu.CompilerParams(vmem_limit_bytes=52 * 2**20),
         cost_estimate=pl.CostEstimate(
-            flops=16_000_000_000, bytes_accessed=20_000_000, transcendentals=8_000_000
+            flops=pairs * 5_000_000_000, bytes_accessed=8_000_000, transcendentals=pairs * 1_400_000
         ),
     )(begins, normed, seed_rows, weight_qkv, bias_qkv, weight_out, *tables)
 
@@ -317,15 +316,23 @@
     normed_two = normed_two.astype(jnp.bfloat16)
     seed_rows = jnp.where(live_rows[:, None], cotangent, jnp.zeros_like(cotangent))
     begins = jnp.arange(TOK_DEV, dtype=jnp.int32) - position
-    context, grad_projected = attention(
-        begins[None, :],
-        normed_one,
-        seed_rows,
-        weight_qkv,
-        bias_qkv[None, :],
-        weight_out,
-        lane_tables(position),
-    )
+    tables = lane_tables(position)
+    parts = [
+        attention(
+            begins[None, :],
+            normed_one,
+            seed_rows,
+            weight_qkv,
+            bias_qkv[None, :],
+            weight_out,
+            tables,
+            first,
+            2,
+        )
+        for first in range(0, HEADS // 2, 2)
+    ]
+    context = jnp.concatenate([part[0] for part in parts], axis=1)
+    grad_projected = jnp.concatenate([part[1] for part in parts], axis=1)
     attended = jnp.dot(context, weight_out, preferred_element_type=jnp.float32) + bias_out
     hidden = jnp.dot(normed_two, weight_up, preferred_element_type=jnp.float32) + bias_up
     activation, gelu_back = jax.vjp(lambda entry: jax.nn.gelu(entry, approximate=False), hidden)

time: 539 us -> 522 us (0.968)
  waiting for transfers between devices: 214 us -> 192 us
  other arithmetic: 63.4 us -> 71.5 us
  Pallas kernels: 76.2 us -> 84.2 us
  matrix products: 104 us -> 96.7 us
  starting transfers between devices: 39.8 us -> 34.4 us
    ppermute x40, waiting for transfers between devices: 214 us -> 192 us  [exchange(): return lax.ppermute(block, ('dp', 'group'), pairs)]
    pallas_call x1 -> x3, Pallas kernels: 76.2 us -> 84.2 us  [attention(): pl.pallas_call(attention_kernel, grid=(pairs,), in_specs=[whole(1, TOK_DE...]
    unnamed x112 -> x124, local copies, waits for them, and re-layouts: 8.13 us -> 12.4 us
  transfers between devices with their start and end apart: 40 -> 40, of which waited for: 23 -> 21; matrix products, arithmetic and copies ran while one was open for 26% -> 27% of each run, Pallas kernels for 14% -> 16%
where the time goes in v3:
time: 522 us; the launch traced here: 514 us
  waiting for transfers between devices  192 us (37%)
  matrix products  96.7 us (19%)
  Pallas kernels  84.2 us (16%)
  other arithmetic  71.5 us (14%)
  starting transfers between devices  34.4 us (7%)
  local copies, waits for them, and re-layouts  32.9 us (6%)
    ppermute x40, waiting for transfers between devices, exchange(): return lax.ppermute(block, ('dp', 'group'), pairs)  192 us
    pallas_call x3, Pallas kernels, attention(): pl.pallas_call(attention_kernel, grid=(pairs,), in_specs=[whole(1, TOK_DE...  84.2 us
    dot_general x1, matrix products, per_device(): jnp.dot(normed_two, weight_up, preferred_element_type=jnp.float32) + bias_up  36.3 us
    ppermute x40, starting transfers between devices, exchange(): return lax.ppermute(block, ('dp', 'group'), pairs)  34.4 us
    another operation x33, other arithmetic, gather_rows(): block = jnp.stack([low, high], axis=1).reshape(-1, columns)  18.5 us
    dot_general x1, matrix products, per_device(): jnp.einsum('td,fd->tf', seed_rows, weight_down, preferred_element_type=jn...  17.1 us
    unnamed x124, local copies, waits for them, and re-layouts  12.4 us
  transfers between devices with their start and end apart: 40, of which 21 were waited for; matrix products, arithmetic and copies ran while one was open for 27% of the time, Pallas kernels for 16%

profile of v3, /device:TPU:0, one launch (start us, length us, event | category | flops | bytes accessed | tf_op | source)
XLA Modules:
  0.0 514.4 jit_solution(11799117594933725501)
XLA Ops:
  19.4 3.0 multiply_sine_fusion
  28.0 14.8 %collective-permute-done.1 = bf16[48,3200]{1,0:T(8,128)(2,1)S(1)} collective-permute-done((bf16[48,3200]{1,0:T(8,128)(2,1)S(1)}, bf16[48,3200]{1,0:T(8,128)(2,1)S(1)}, u32[]{:S(2)}, u32[]{:S(2)}) %collective-permute-start.1) | collective-permute-done | bytes 307232 | tf_op jit(solution)/shard_map/ppermute | solution.py:203
  45.7 13.1 %collective-permute-done.2 = bf16[96,3200]{1,0:T(8,128)(2,1)S(1)} collective-permute-done((bf16[96,3200]{1,0:T(8,128)(2,1)S(1)}, bf16[96,3200]{1,0:T(8,128)(2,1)S(1)}, u32[]{:S(2)}, u32[]{:S(2)}) %collective-permute-start.2) | collective-permute-done | bytes 614432 | tf_op jit(solution)/shard_map/ppermute | solution.py:203
  75.7 14.6 %collective-permute-done.3 = bf16[192,3200]{1,0:T(8,128)(2,1)} collective-permute-done((bf16[192,3200]{1,0:T(8,128)(2,1)}, bf16[192,3200]{1,0:T(8,128)(2,1)}, u32[]{:S(2)}, u32[]{:S(2)}) %collective-permute-start.3) | collective-permute-done | bytes 1228832 | tf_op jit(solution)/shard_map/ppermute | solution.py:203
  96.4 12.1 %collective-permute-done.8 = bf16[192,1536]{1,0:T(8,128)(2,1)S(1)} collective-permute-done((bf16[192,1536]{1,0:T(8,128)(2,1)S(1)}, bf16[192,1536]{1,0:T(8,128)(2,1)S(1)}, u32[]{:S(2)}, u32[]{:S(2)}) %collective-permute-start.8) | collective-permute-done | bytes 589856 | tf_op jit(solution)/shard_map/ppermute | solution.py:203
  115.7 36.3 %multiply_convert_fusion = (bf16[1024,3072]{1,0:T(8,128)(2,1)S(1)}, f32[1024,3072]{1,0:T(8,128)}, f32[1024,3072]{1,0:T(8,128)}) fusion(f32[3072]{0:T(1024)S(1)} %slice.95, bf16[768,3200]{1,0:T(8,128)(2,1)} %bitcast.273, bf16[1024,768]{1,0:T(8,128)(2,1)S(1)} %copy-done, f32[768]{0:T(1024)S(1)} %get-tuple-element.107, f32[768]{0:T(1024)S(1)} %get-tuple-element.108, ...), kind=kOutput, calls=%fused_computation.3 | convolution fusion | flops 5044174848 | bytes 37775360 | tf_op jit(solution)/shard_map/dot_general | solution.py:337
  152.1 5.6 %convolution_convert_fusion = bf16[3072,768]{1,0:T(8,128)(2,1)S(1)} fusion(bf16[1024,3072]{1,0:T(8,128)(2,1)S(1)} %get-tuple-element.58, bf16[1024,768]{1,0:T(8,128)(2,1)S(1)} %copy-done.9), kind=kOutput, calls=%fused_computation.19 | convolution fusion | flops 4834197504 | bytes 12582912 | tf_op jit(solution)/shard_map/tf,td->fd/dot_general | solution.py:347
  171.9 27.9 %shard_map.305 = (bf16[1024,256]{1,0:T(8,128)(2,1)S(1)}, bf16[1024,768]{1,0:T(8,128)(2,1)}) custom-call(s32[1,1024]{1,0:T(1,128)S(1)} %subtract_subtract_fusion.begins_ref, bf16[1024,768]{1,0:T(8,128)(2,1)} %fusion.24.normed_ref, bf16[1024,768]{1,0:T(8,128)(2,1)} %get-tuple-element.57.seed_ref, bf16[768,2304]{1,0:T(8,128)(2,1)} %pad_maximum_fusion.2.weight_ref, ...), custom_call_target="tpu_custom_call" | custom-call | flops 10000000000 | bytes 8000000 | tf_op jit(solution)/shard_map/pallas_call | solution.py:171
  201.3 28.1 %shard_map.306 = (bf16[1024,256]{1,0:T(8,128)(2,1)S(1)}, bf16[1024,768]{1,0:T(8,128)(2,1)}) custom-call(s32[1,1024]{1,0:T(1,128)S(1)} %subtract_subtract_fusion.begins_ref, bf16[1024,768]{1,0:T(8,128)(2,1)} %fusion.24.normed_ref, bf16[1024,768]{1,0:T(8,128)(2,1)} %get-tuple-element.57.seed_ref, bf16[768,2304]{1,0:T(8,128)(2,1)} %pad_maximum_fusion.2.weight_ref, ...), custom_call_target="tpu_custom_call" | custom-call | flops 10000000000 | bytes 8000000 | tf_op jit(solution)/shard_map/pallas_call | solution.py:171
  232.5 28.2 %shard_map.307 = (bf16[1024,256]{1,0:T(8,128)(2,1)S(1)}, bf16[1024,768]{1,0:T(8,128)(2,1)}) custom-call(s32[1,1024]{1,0:T(1,128)S(1)} %subtract_subtract_fusion.begins_ref, bf16[1024,768]{1,0:T(8,128)(2,1)} %fusion.24.normed_ref, bf16[1024,768]{1,0:T(8,128)(2,1)} %get-tuple-element.57.seed_ref, bf16[768,2304]{1,0:T(8,128)(2,1)} %pad_maximum_fusion.2.weight_ref, ...), custom_call_target="tpu_custom_call" | custom-call | flops 10000000000 | bytes 8000000 | tf_op jit(solution)/shard_map/pallas_call | solution.py:171
  262.7 12.2 %collective-permute-done.38 = bf16[1,192,768]{2,1,0:T(8,128)(2,1)S(1)} collective-permute-done((bf16[1,192,768]{2,1,0:T(8,128)(2,1)S(1)}, bf16[1,192,768]{2,1,0:T(8,128)(2,1)S(1)}, u32[]{:S(2)}, u32[]{:S(2)}) %collective-permute-start.38) | collective-permute-done | bytes 294944 | tf_op jit(solution)/shard_map/ppermute | solution.py:203
  275.1 4.4 convolution_convert_fusion.2
  291.8 12.8 %collective-permute-done.16 = bf16[192,768]{1,0:T(8,128)(2,1)S(1)} collective-permute-done((bf16[192,768]{1,0:T(8,128)(2,1)S(1)}, bf16[192,768]{1,0:T(8,128)(2,1)S(1)}, u32[]{:S(2)}, u32[]{:S(2)}) %collective-permute-start.16) | collective-permute-done | bytes 294944 | tf_op jit(solution)/shard_map/ppermute | solution.py:203
  308.2 12.8 %collective-permute-done.17 = bf16[384,768]{1,0:T(8,128)(2,1)S(1)} collective-permute-done((bf16[384,768]{1,0:T(8,128)(2,1)S(1)}, bf16[384,768]{1,0:T(8,128)(2,1)S(1)}, u32[]{:S(2)}, u32[]{:S(2)}) %collective-permute-start.17) | collective-permute-done | bytes 589856 | tf_op jit(solution)/shard_map/ppermute | solution.py:203
  322.9 9.0 %collective-permute-done.21 = bf16[2,96,1536]{2,1,0:T(8,128)(2,1)} collective-permute-done((bf16[2,96,1536]{2,1,0:T(8,128)(2,1)S(1)}, bf16[2,96,1536]{2,1,0:T(8,128)(2,1)}, u32[]{:S(2)}, u32[]{:S(2)}) %collective-permute-start.21) | collective-permute-done | bytes 589856 | tf_op jit(solution)/shard_map/ppermute | solution.py:203
  333.9 16.1 %collective-permute-done.18 = bf16[768,768]{1,0:T(8,128)(2,1)} collective-permute-done((bf16[768,768]{1,0:T(8,128)(2,1)}, bf16[768,768]{1,0:T(8,128)(2,1)}, u32[]{:S(2)}, u32[]{:S(2)}) %collective-permute-start.18) | collective-permute-done | bytes 1179680 | tf_op jit(solution)/shard_map/ppermute | solution.py:203
  356.2 7.2 %collective-permute-done.23 = bf16[1,48,1536]{2,1,0:T(8,128)(2,1)S(1)} collective-permute-done((bf16[1,48,1536]{2,1,0:T(8,128)(2,1)S(1)}, bf16[1,48,1536]{2,1,0:T(8,128)(2,1)S(1)}, u32[]{:S(2)}, u32[]{:S(2)}) %collective-permute-start.23) | collective-permute-done | bytes 147488 | tf_op jit(solution)/shard_map/ppermute | solution.py:203
  363.6 3.1 fusion.65
  369.0 3.0 reduce
  377.6 17.1 %fusion.80 = (bf16[3072]{0:T(1024)(128)(2,1)S(1)}, bf16[1024,3072]{1,0:T(8,128)(2,1)}) fusion(f32[1024,3072]{1,0:T(8,128)} %get-tuple-element.59, bf16[1024,768]{1,0:T(8,128)(2,1)S(1)} %copy-done.10, bf16[3072,768]{1,0:T(8,128)(2,1)} %bitcast.283, f32[1024,3072]{1,0:T(8,128)} %get-tuple-element.114, f32[3072]{0:T(1024)S(1)} %copy-done.38), kind=kOutput, calls=%fused_computation.236 | convolution fusion | flops 4882166784 | bytes 37767168 | tf_op jit(solution)/shard_map/td,fd->tf/dot_general | solution.py:349
  394.7 8.7 %fusion.9 = f32[1024,768]{1,0:T(8,128)S(1)} fusion(bf16[1024,3072]{1,0:T(8,128)(2,1)} %get-tuple-element.117, bf16[768,3200]{1,0:T(8,128)(2,1)} %bitcast.274), kind=kOutput, calls=%fused_computation.31 | convolution fusion | flops 4831838208 | bytes 14155776 | tf_op jit(solution)/shard_map/tf,df->td/dot_general | solution.py:352
  403.6 6.3 %fusion.35 = (bf16[768]{0:T(1024)(128)(2,1)S(1)}, f32[1024]{0:T(1024)S(1)}, f32[1024]{0:T(1024)S(1)}, bf16[768]{0:T(1024)(128)(2,1)S(1)}, bf16[768]{0:T(1024)(12...) fusion(bf16[1024,768]{1,0:T(8,128)(2,1)S(1)} %copy-done.1, ...), kind=kOutput, calls=%fused_computation.58 | convolution fusion | flops 3644318720 | bytes 16158720 | tf_op jit(solution)/shard_map/te,de->td/dot_general | solution.py:356
  415.1 6.3 %convolution_convert_fusion.1 = bf16[768,3072]{1,0:T(8,128)(2,1)S(1)} fusion(bf16[1024,3072]{1,0:T(8,128)(2,1)S(1)} %copy-done.48, bf16[1024,768]{1,0:T(8,128)(2,1)S(1)} %copy-done.1, f32[768]{0:T(1024)S(1)} %copy-done.43, f32[768]{0:T(1024)S(1)} %get-tuple-element.108, f32[1024]{0:T(1024)S(1)} %copy-done.34, f32[1024]{0:T(1024)S(1)} %broadcast_multiply_fusion.4), kind=kOutput, calls=%fused_computation.20 | convolution fusion | flops 4838916096 | bytes 12597248 | tf_op jit(solution)/shard_map/td,tf->df/dot_general | solution.py:351
  423.5 6.4 %fusion.40 = bf16[1024,768]{1,0:T(8,128)(2,1)} fusion(bf16[1024,768]{1,0:T(8,128)(2,1)S(1)} %copy-done.1, f32[1024,768]{1,0:T(8,128)S(1)} %copy-done.47, bf16[1024,3072]{1,0:T(8,128)(2,1)S(1)} %bitcast.330, bf16[3072,768]{1,0:T(8,128)(2,1)S(1)} %bitcast.286, f32[768]{0:T(1024)S(1)} %copy-done.41, f32[768]{0:T(1024)S(1)} %copy-done.40), kind=kOutput, calls=%fused_computation.63 | convolution fusion | flops 4836556800 | bytes 17307648 | tf_op jit(solution)/shard_map/dot_general | solution.py:343
  429.9 9.0 %collective-permute-done.26 = bf16[1,192,1664]{2,1,0:T(8,128)(2,1)S(1)} collective-permute-done((bf16[1,192,1664]{2,1,0:T(8,128)(2,1)S(1)}, bf16[1,192,1664]{2,1,0:T(8,128)(2,1)S(1)}, u32[]{:S(2)}, u32[]{:S(2)}) %collective-permute-start.26) | collective-permute-done | bytes 639008 | tf_op jit(solution)/shard_map/ppermute | solution.py:203
  439.8 8.5 %collective-permute-done.27 = bf16[1,96,1664]{2,1,0:T(8,128)(2,1)S(1)} collective-permute-done((bf16[1,96,1664]{2,1,0:T(8,128)(2,1)S(1)}, bf16[1,96,1664]{2,1,0:T(8,128)(2,1)S(1)}, u32[]{:S(2)}, u32[]{:S(2)}) %collective-permute-start.27) | collective-permute-done | bytes 319520 | tf_op jit(solution)/shard_map/ppermute | solution.py:203
  452.4 5.3 %collective-permute-done.28 = bf16[1,48,1664]{2,1,0:T(8,128)(2,1)S(1)} collective-permute-done((bf16[1,48,1664]{2,1,0:T(8,128)(2,1)S(1)}, bf16[1,48,1664]{2,1,0:T(8,128)(2,1)S(1)}, u32[]{:S(2)}, u32[]{:S(2)}) %collective-permute-start.28) | collective-permute-done | bytes 159776 | tf_op jit(solution)/shard_map/ppermute | solution.py:203
  457.9 3.3 fusion.31
  463.0 15.4 %collective-permute-done.31 = bf16[2,96,3072]{2,1,0:T(8,128)(2,1)} collective-permute-done((bf16[2,96,3072]{2,1,0:T(8,128)(2,1)S(1)}, bf16[2,96,3072]{2,1,0:T(8,128)(2,1)}, u32[]{:S(2)}, u32[]{:S(2)}) %collective-permute-start.31) | collective-permute-done | bytes 1179680 | tf_op jit(solution)/shard_map/ppermute | solution.py:203
  483.1 10.4 %collective-permute-done.32 = bf16[1,96,3072]{2,1,0:T(8,128)(2,1)S(1)} collective-permute-done((bf16[1,96,3072]{2,1,0:T(8,128)(2,1)S(1)}, bf16[1,96,3072]{2,1,0:T(8,128)(2,1)S(1)}, u32[]{:S(2)}, u32[]{:S(2)}) %collective-permute-start.32) | collective-permute-done | bytes 589856 | tf_op jit(solution)/shard_map/ppermute | solution.py:203
  496.0 10.5 %collective-permute-done.33 = bf16[1,48,3072]{2,1,0:T(8,128)(2,1)S(1)} collective-permute-done((bf16[1,48,3072]{2,1,0:T(8,128)(2,1)S(1)}, bf16[1,48,3072]{2,1,0:T(8,128)(2,1)S(1)}, u32[]{:S(2)}, u32[]{:S(2)}) %collective-permute-start.33) | collective-permute-done | bytes 294944 | tf_op jit(solution)/shard_map/ppermute | solution.py:203
  507.3 4.5 collective-permute-done.34
  (334 shorter events, 136.0 us)
Async XLA Ops:
  3.4 19.7 %collective-permute-start = (bf16[24,3200]{1,0:T(8,128)(2,1)}, bf16[24,3200]{1,0:T(8,128)(2,1)}, u32[]{:S(2)}, u32[]{:S(2)}) collective-permute-start(bf16[24,3200]{1,0:T(8,128)(2,1)} %fusion.61), channel_id=1, source_target_pairs={{0,1},{1,0},{2,3},{3,2},{4,5},{5,4},{6,7},{7,6},{8,9},{9,8},{10,11... | collective-permute-start | bytes 460808 | tf_op jit(solution)/shard_map/ppermute | solution.py:203
  9.1 17.6 %collective-permute-start.10 = (bf16[24,1536]{1,0:T(8,128)(2,1)}, bf16[24,1536]{1,0:T(8,128)(2,1)}, u32[]{:S(2)}, u32[]{:S(2)}) collective-permute-start(bf16[24,1536]{1,0:T(8,128)(2,1)} %pad_maximum_fusion.22), channel_id=1, source_target_pairs={{0,1},{1,0},{2,3},{3,2},{4,5},{5,4},{6,7},{7,6},{8,9},{9,8},{10,11... | collective-permute-start | bytes 221192 | tf_op jit(solution)/shard_map/ppermute | solution.py:203
  9.1 35.5 %collective-permute-start.5 = (bf16[24,1536]{1,0:T(8,128)(2,1)S(1)}, bf16[24,1536]{1,0:T(8,128)(2,1)}, u32[]{:S(2)}, u32[]{:S(2)}) collective-permute-start(bf16[24,1536]{1,0:T(8,128)(2,1)S(1)} %slice.86), channel_id=1, source_target_pairs={{0,1},{1,0},{2,3},{3,2},{4,5},{5,4},{6,7},{7,6},{8,9},{9,8},{10,11... | collective-permute-start | bytes 221192 | tf_op jit(solution)/shard_map/ppermute | solution.py:203
  24.0 18.8 %collective-permute-start.1 = (bf16[48,3200]{1,0:T(8,128)(2,1)S(1)}, bf16[48,3200]{1,0:T(8,128)(2,1)S(1)}, u32[]{:S(2)}, u32[]{:S(2)}) collective-permute-start(bf16[48,3200]{1,0:T(8,128)(2,1)S(1)} %bitcast.309), channel_id=1, source_target_pairs={{0,2},{1,3},{2,0},{3,1},{4,6},{5,7},{6,4},{7,5},{8,10},{9,11},{10,... | collective-permute-start | bytes 921608 | tf_op jit(solution)/shard_map/ppermute | solution.py:203
  27.6 34.0 %collective-permute-start.11 = (bf16[48,1536]{1,0:T(8,128)(2,1)S(1)}, bf16[48,1536]{1,0:T(8,128)(2,1)S(1)}, u32[]{:S(2)}, u32[]{:S(2)}) collective-permute-start(bf16[48,1536]{1,0:T(8,128)(2,1)S(1)} %bitcast.322), channel_id=1, source_target_pairs={{0,2},{1,3},{2,0},{3,1},{4,6},{5,7},{6,4},{7,5},{8,10},{9,11},{10,... | collective-permute-start | bytes 442376 | tf_op jit(solution)/shard_map/ppermute | solution.py:203
  43.0 15.7 %collective-permute-start.2 = (bf16[96,3200]{1,0:T(8,128)(2,1)S(1)}, bf16[96,3200]{1,0:T(8,128)(2,1)S(1)}, u32[]{:S(2)}, u32[]{:S(2)}) collective-permute-start(bf16[96,3200]{1,0:T(8,128)(2,1)S(1)} %bitcast.297), channel_id=1, source_target_pairs={{0,16},{1,17},{2,18},{3,19},{4,20},{5,21},{6,22},{7,23},{8,24},{9,... | collective-permute-start | bytes 1843208 | tf_op jit(solution)/shard_map/ppermute | solution.py:203
  45.6 16.1 %collective-permute-start.6 = (bf16[48,1536]{1,0:T(8,128)(2,1)S(1)}, bf16[48,1536]{1,0:T(8,128)(2,1)S(1)}, u32[]{:S(2)}, u32[]{:S(2)}) collective-permute-start(bf16[48,1536]{1,0:T(8,128)(2,1)S(1)} %bitcast.323), channel_id=1, source_target_pairs={{0,2},{1,3},{2,0},{3,1},{4,6},{5,7},{6,4},{7,5},{8,10},{9,11},{10,... | collective-permute-start | bytes 442376 | tf_op jit(solution)/shard_map/ppermute | solution.py:203
  60.1 30.3 %collective-permute-start.3 = (bf16[192,3200]{1,0:T(8,128)(2,1)}, bf16[192,3200]{1,0:T(8,128)(2,1)}, u32[]{:S(2)}, u32[]{:S(2)}) collective-permute-start(bf16[192,3200]{1,0:T(8,128)(2,1)} %bitcast.11), channel_id=1, source_target_pairs={{0,8},{1,9},{2,10},{3,11},{4,12},{5,13},{6,14},{7,15},{8,0},{9,1},... | collective-permute-start | bytes 3686408 | tf_op jit(solution)/shard_map/ppermute | solution.py:203
  62.4 12.3 %collective-permute-start.7 = (bf16[96,1536]{1,0:T(8,128)(2,1)S(1)}, bf16[96,1536]{1,0:T(8,128)(2,1)}, u32[]{:S(2)}, u32[]{:S(2)}) collective-permute-start(bf16[96,1536]{1,0:T(8,128)(2,1)S(1)} %bitcast.316), channel_id=1, source_target_pairs={{0,16},{1,17},{2,18},{3,19},{4,20},{5,21},{6,22},{7,23},{8,24},{9,... | collective-permute-start | bytes 884744 | tf_op jit(solution)/shard_map/ppermute | solution.py:203
  74.1 20.5 %collective-permute-start.12 = (bf16[96,1536]{1,0:T(8,128)(2,1)S(1)}, bf16[96,1536]{1,0:T(8,128)(2,1)S(1)}, u32[]{:S(2)}, u32[]{:S(2)}) collective-permute-start(bf16[96,1536]{1,0:T(8,128)(2,1)S(1)} %bitcast.317), channel_id=1, source_target_pairs={{0,8},{1,9},{2,10},{3,11},{4,12},{5,13},{6,14},{7,15},{8,0},{9,1},... | collective-permute-start | bytes 884744 | tf_op jit(solution)/shard_map/ppermute | solution.py:203
  92.5 18.9 %collective-permute-start.4 = (bf16[384,3200]{1,0:T(8,128)(2,1)S(1)}, bf16[384,3200]{1,0:T(8,128)(2,1)S(1)}, u32[]{:S(2)}, u32[]{:S(2)}) collective-permute-start(bf16[384,3200]{1,0:T(8,128)(2,1)S(1)} %bitcast.255), channel_id=1, source_target_pairs={{0,4},{1,5},{2,6},{3,7},{4,0},{5,1},{6,2},{7,3},{8,12},{9,13},{10,... | collective-permute-start | bytes 7372808 | tf_op jit(solution)/shard_map/ppermute | solution.py:203
  92.6 15.8 %collective-permute-start.8 = (bf16[192,1536]{1,0:T(8,128)(2,1)S(1)}, bf16[192,1536]{1,0:T(8,128)(2,1)S(1)}, u32[]{:S(2)}, u32[]{:S(2)}) collective-permute-start(bf16[192,1536]{1,0:T(8,128)(2,1)S(1)} %bitcast.298), channel_id=1, source_target_pairs={{0,8},{1,9},{2,10},{3,11},{4,12},{5,13},{6,14},{7,15},{8,0},{9,1},... | collective-permute-start | bytes 1769480 | tf_op jit(solution)/shard_map/ppermute | solution.py:203
  94.7 15.2 %collective-permute-start.13 = (bf16[192,1536]{1,0:T(8,128)(2,1)S(1)}, bf16[192,1536]{1,0:T(8,128)(2,1)S(1)}, u32[]{:S(2)}, u32[]{:S(2)}) collective-permute-start(bf16[192,1536]{1,0:T(8,128)(2,1)S(1)} %bitcast.299), channel_id=1, source_target_pairs={{0,16},{1,17},{2,18},{3,19},{4,20},{5,21},{6,22},{7,23},{8,24},{9,... | collective-permute-start | bytes 1769480 | tf_op jit(solution)/shard_map/ppermute | solution.py:203
  109.7 48.5 %collective-permute-start.9 = (bf16[384,1536]{1,0:T(8,128)(2,1)}, bf16[384,1536]{1,0:T(8,128)(2,1)}, u32[]{:S(2)}, u32[]{:S(2)}) collective-permute-start(bf16[384,1536]{1,0:T(8,128)(2,1)} %bitcast.30), channel_id=1, source_target_pairs={{0,4},{1,5},{2,6},{3,7},{4,0},{5,1},{6,2},{7,3},{8,12},{9,13},{10,... | collective-permute-start | bytes 3538952 | tf_op jit(solution)/shard_map/ppermute | solution.py:203
  111.1 49.1 %collective-permute-start.14 = (bf16[384,1536]{1,0:T(8,128)(2,1)}, bf16[384,1536]{1,0:T(8,128)(2,1)}, u32[]{:S(2)}, u32[]{:S(2)}) collective-permute-start(bf16[384,1536]{1,0:T(8,128)(2,1)} %bitcast.45), channel_id=1, source_target_pairs={{0,4},{1,5},{2,6},{3,7},{4,0},{5,1},{6,2},{7,3},{8,12},{9,13},{10,... | collective-permute-start | bytes 3538952 | tf_op jit(solution)/shard_map/ppermute | solution.py:203
  157.9 11.7 %collective-permute-start.35 = (bf16[4,384,768]{2,1,0:T(8,128)(2,1)S(1)}, bf16[4,384,768]{2,1,0:T(8,128)(2,1)S(1)}, u32[]{:S(2)}, u32[]{:S(2)}) collective-permute-start(bf16[4,384,768]{2,1,0:T(8,128)(2,1)S(1)} %dynamic-slice_bitcast_fusion), channel_id=1, source_target_pairs={{0,4},{1,5},{2,6},{3,7},{4,0},{5,1},{6,2},{7,3},{8,12},{9,13},{10,... | collective-permute-start | bytes 7077896 | tf_op jit(solution)/shard_map/ppermute | solution.py:203
  170.3 59.0 %collective-permute-start.36 = (bf16[1,768,768]{2,1,0:T(8,128)(2,1)S(1)}, bf16[1,768,768]{2,1,0:T(8,128)(2,1)}, u32[]{:S(2)}, u32[]{:S(2)}) collective-permute-start(bf16[1,768,768]{2,1,0:T(8,128)(2,1)S(1)} %dynamic-slice_bitcast_fusion.3), channel_id=1, source_target_pairs={{0,16},{1,17},{2,18},{3,19},{4,20},{5,21},{6,22},{7,23},{8,24},{9,... | collective-permute-start | bytes 3538952 | tf_op jit(solution)/shard_map/ppermute | solution.py:203
  231.0 29.6 %collective-permute-start.37 = (bf16[1,384,768]{2,1,0:T(8,128)(2,1)S(1)}, bf16[1,384,768]{2,1,0:T(8,128)(2,1)S(1)}, u32[]{:S(2)}, u32[]{:S(2)}) collective-permute-start(bf16[1,384,768]{2,1,0:T(8,128)(2,1)S(1)} %dynamic-slice_bitcast_fusion.7), channel_id=1, source_target_pairs={{0,8},{1,9},{2,10},{3,11},{4,12},{5,13},{6,14},{7,15},{8,0},{9,1},... | collective-permute-start | bytes 1769480 | tf_op jit(solution)/shard_map/ppermute | solution.py:203
  260.9 14.0 %collective-permute-start.38 = (bf16[1,192,768]{2,1,0:T(8,128)(2,1)S(1)}, bf16[1,192,768]{2,1,0:T(8,128)(2,1)S(1)}, u32[]{:S(2)}, u32[]{:S(2)}) collective-permute-start(bf16[1,192,768]{2,1,0:T(8,128)(2,1)S(1)} %dynamic-slice_bitcast_fusion.10), channel_id=1, source_target_pairs={{0,2},{1,3},{2,0},{3,1},{4,6},{5,7},{6,4},{7,5},{8,10},{9,11},{10,... | collective-permute-start | bytes 884744 | tf_op jit(solution)/shard_map/ppermute | solution.py:203
  286.7 18.6 %collective-permute-start.20 = (bf16[4,96,1536]{2,1,0:T(8,128)(2,1)S(1)}, bf16[4,96,1536]{2,1,0:T(8,128)(2,1)S(1)}, u32[]{:S(2)}, u32[]{:S(2)}) collective-permute-start(bf16[4,96,1536]{2,1,0:T(8,128)(2,1)S(1)} %dynamic-slice_bitcast_fusion.5), channel_id=1, source_target_pairs={{0,4},{1,5},{2,6},{3,7},{4,0},{5,1},{6,2},{7,3},{8,12},{9,13},{10,... | collective-permute-start | bytes 3538952 | tf_op jit(solution)/shard_map/ppermute | solution.py:203
  289.2 15.4 %collective-permute-start.16 = (bf16[192,768]{1,0:T(8,128)(2,1)S(1)}, bf16[192,768]{1,0:T(8,128)(2,1)S(1)}, u32[]{:S(2)}, u32[]{:S(2)}) collective-permute-start(bf16[192,768]{1,0:T(8,128)(2,1)S(1)} %bitcast.318), channel_id=1, source_target_pairs={{0,2},{1,3},{2,0},{3,1},{4,6},{5,7},{6,4},{7,5},{8,10},{9,11},{10,... | collective-permute-start | bytes 884744 | tf_op jit(solution)/shard_map/ppermute | solution.py:203
  304.7 16.3 %collective-permute-start.17 = (bf16[384,768]{1,0:T(8,128)(2,1)S(1)}, bf16[384,768]{1,0:T(8,128)(2,1)S(1)}, u32[]{:S(2)}, u32[]{:S(2)}) collective-permute-start(bf16[384,768]{1,0:T(8,128)(2,1)S(1)} %bitcast.300), channel_id=1, source_target_pairs={{0,8},{1,9},{2,10},{3,11},{4,12},{5,13},{6,14},{7,15},{8,0},{9,1},... | collective-permute-start | bytes 1769480 | tf_op jit(solution)/shard_map/ppermute | solution.py:203
  306.7 25.2 %collective-permute-start.21 = (bf16[2,96,1536]{2,1,0:T(8,128)(2,1)S(1)}, bf16[2,96,1536]{2,1,0:T(8,128)(2,1)}, u32[]{:S(2)}, u32[]{:S(2)}) collective-permute-start(bf16[2,96,1536]{2,1,0:T(8,128)(2,1)S(1)} %dynamic-slice_bitcast_fusion.8), channel_id=1, source_target_pairs={{0,8},{1,9},{2,10},{3,11},{4,12},{5,13},{6,14},{7,15},{8,0},{9,1},... | collective-permute-start | bytes 1769480 | tf_op jit(solution)/shard_map/ppermute | solution.py:203
  322.3 27.7 %collective-permute-start.18 = (bf16[768,768]{1,0:T(8,128)(2,1)}, bf16[768,768]{1,0:T(8,128)(2,1)}, u32[]{:S(2)}, u32[]{:S(2)}) collective-permute-start(bf16[768,768]{1,0:T(8,128)(2,1)} %bitcast.57), channel_id=1, source_target_pairs={{0,16},{1,17},{2,18},{3,19},{4,20},{5,21},{6,22},{7,23},{8,24},{9,... | collective-permute-start | bytes 3538952 | tf_op jit(solution)/shard_map/ppermute | solution.py:203
  333.3 20.1 %collective-permute-start.22 = (bf16[1,96,1536]{2,1,0:T(8,128)(2,1)S(1)}, bf16[1,96,1536]{2,1,0:T(8,128)(2,1)S(1)}, u32[]{:S(2)}, u32[]{:S(2)}) collective-permute-start(bf16[1,96,1536]{2,1,0:T(8,128)(2,1)S(1)} %constant_dynamic-slice_fusion.1), channel_id=1, source_target_pairs={{0,16},{1,17},{2,18},{3,19},{4,20},{5,21},{6,22},{7,23},{8,24},{9,... | collective-permute-start | bytes 884744 | tf_op jit(solution)/shard_map/ppermute | solution.py:203
  353.4 18.7 %collective-permute-start.19 = (bf16[1536,768]{1,0:T(8,128)(2,1)}, bf16[1536,768]{1,0:T(8,128)(2,1)}, u32[]{:S(2)}, u32[]{:S(2)}) collective-permute-start(bf16[1536,768]{1,0:T(8,128)(2,1)} %bitcast.60), channel_id=1, source_target_pairs={{0,4},{1,5},{2,6},{3,7},{4,0},{5,1},{6,2},{7,3},{8,12},{9,13},{10,... | collective-permute-start | bytes 7077896 | tf_op jit(solution)/shard_map/ppermute | solution.py:203
  353.5 9.9 %collective-permute-start.23 = (bf16[1,48,1536]{2,1,0:T(8,128)(2,1)S(1)}, bf16[1,48,1536]{2,1,0:T(8,128)(2,1)S(1)}, u32[]{:S(2)}, u32[]{:S(2)}) collective-permute-start(bf16[1,48,1536]{2,1,0:T(8,128)(2,1)S(1)} %dynamic-slice_bitcast_fusion.15), channel_id=1, source_target_pairs={{0,2},{1,3},{2,0},{3,1},{4,6},{5,7},{6,4},{7,5},{8,10},{9,11},{10,... | collective-permute-start | bytes 442376 | tf_op jit(solution)/shard_map/ppermute | solution.py:203
  421.6 29.2 %collective-permute-start.30 = (bf16[4,96,3072]{2,1,0:T(8,128)(2,1)S(1)}, bf16[4,96,3072]{2,1,0:T(8,128)(2,1)S(1)}, u32[]{:S(2)}, u32[]{:S(2)}) collective-permute-start(bf16[4,96,3072]{2,1,0:T(8,128)(2,1)S(1)} %dynamic-slice_bitcast_fusion.1), channel_id=1, source_target_pairs={{0,4},{1,5},{2,6},{3,7},{4,0},{5,1},{6,2},{7,3},{8,12},{9,13},{10,... | collective-permute-start | bytes 7077896 | tf_op jit(solution)/shard_map/ppermute | solution.py:203
  422.1 16.8 %collective-permute-start.26 = (bf16[1,192,1664]{2,1,0:T(8,128)(2,1)S(1)}, bf16[1,192,1664]{2,1,0:T(8,128)(2,1)S(1)}, u32[]{:S(2)}, u32[]{:S(2)}) collective-permute-start(bf16[1,192,1664]{2,1,0:T(8,128)(2,1)S(1)} %dynamic-slice_bitcast_fusion.6), channel_id=1, source_target_pairs={{0,16},{1,17},{2,18},{3,19},{4,20},{5,21},{6,22},{7,23},{8,24},{9,... | collective-permute-start | bytes 1916936 | tf_op jit(solution)/shard_map/ppermute | solution.py:203
  451.8 26.6 %collective-permute-start.31 = (bf16[2,96,3072]{2,1,0:T(8,128)(2,1)S(1)}, bf16[2,96,3072]{2,1,0:T(8,128)(2,1)}, u32[]{:S(2)}, u32[]{:S(2)}) collective-permute-start(bf16[2,96,3072]{2,1,0:T(8,128)(2,1)S(1)} %dynamic-slice_bitcast_fusion.4), channel_id=1, source_target_pairs={{0,8},{1,9},{2,10},{3,11},{4,12},{5,13},{6,14},{7,15},{8,0},{9,1},... | collective-permute-start | bytes 3538952 | tf_op jit(solution)/shard_map/ppermute | solution.py:203
  480.6 12.9 %collective-permute-start.32 = (bf16[1,96,3072]{2,1,0:T(8,128)(2,1)S(1)}, bf16[1,96,3072]{2,1,0:T(8,128)(2,1)S(1)}, u32[]{:S(2)}, u32[]{:S(2)}) collective-permute-start(bf16[1,96,3072]{2,1,0:T(8,128)(2,1)S(1)} %constant_dynamic-slice_fusion), channel_id=1, source_target_pairs={{0,16},{1,17},{2,18},{3,19},{4,20},{5,21},{6,22},{7,23},{8,24},{9,... | collective-permute-start | bytes 1769480 | tf_op jit(solution)/shard_map/ppermute | solution.py:203
  493.7 12.8 %collective-permute-start.33 = (bf16[1,48,3072]{2,1,0:T(8,128)(2,1)S(1)}, bf16[1,48,3072]{2,1,0:T(8,128)(2,1)S(1)}, u32[]{:S(2)}, u32[]{:S(2)}) collective-permute-start(bf16[1,48,3072]{2,1,0:T(8,128)(2,1)S(1)} %dynamic-slice_bitcast_fusion.11), channel_id=1, source_target_pairs={{0,2},{1,3},{2,0},{3,1},{4,6},{5,7},{6,4},{7,5},{8,10},{9,11},{10,... | collective-permute-start | bytes 884744 | tf_op jit(solution)/shard_map/ppermute | solution.py:203
  (64 other events, 671.6 us)
